TPU v7x, 512 devices: a whole 4x8x8 slice. The times are simulated.
512 devices in a mesh: wide: 32 (over x, y), narrow: 16 (over z, core).
Axes of the slice: x: 4, y: 8, z: 8, core: 2. Of those that a mesh axis runs over, the one named last changes fastest.
Arguments:
- residual: float32 [3, 512, 256, 128], P(None, 'wide', 'narrow'), may hold values from -6 to 6
- stiffness: float32 [512, 256, 128], P('wide', 'narrow'), may hold values from 0.5 to 4
- coupling: float32 [3, 3], replicated, may hold values from -0.25 to 1.5, as said below
Outputs:
- correction: float32 [3, 512, 256, 128], P(None, 'wide', 'narrow')
Inputs may be any that keep to these rules, and one draw needn't show every extreme that they name: The coupling matrix is symmetric, its diagonal entries lie between 1 and 1.5 and its off-diagonal entries between -0.25 and 0.25.
All inputs are finite; a program needn't handle non-finite values.
Results may differ from a plain program's by a relative error of at most 0.0001.
Values sent between devices are 32-bit elements; how exact they have to be, the bound alone decides.
A program may use at most 128 MiB of HBM per device.

v0:
```python
import functools

import jax
import jax.numpy as jnp
from jax import lax
from jax.experimental import pallas as pl
from jax.experimental.pallas import tpu as pltpu
from jax.sharding import PartitionSpec as P

LEVELS = 4
MASS = 0.001
RATIO = 8.0
MESH = pl.DeviceIdType.MESH
NEIGHBOURS = [(1, 0), (-1, 0), (0, 1), (0, -1), (1, 1), (1, -1), (-1, 1), (-1, -1)]
WINDOW = [o for k in range(1, 6) for o in (k, -k)]
F32 = jnp.float32
BF16 = jnp.bfloat16


def chebyshev(level):
    top = 4.0 * (2.8 / 4.0**level + MASS)
    theta = (top + top / RATIO) / 2.0
    delta = (top - top / RATIO) / 2.0
    sigma = theta / delta
    rho = 1.0 / sigma
    steps = []
    for _ in range(3):
        nxt = 1.0 / (2.0 * sigma - rho)
        steps.append((nxt * rho, 2.0 * nxt / delta))
        rho = nxt
    return theta, steps


def iota(shape, dim):
    return lax.broadcasted_iota(jnp.int32, shape, dim)


def indicator(cond, value=1.0):
    return jnp.where(cond, value, 0.0).astype(BF16)


def mm(v, w):
    hi = v.astype(BF16)
    lo = (v - hi.astype(F32)).astype(BF16)
    return jnp.dot(hi, w, preferred_element_type=F32) + jnp.dot(
        lo, w, preferred_element_type=F32
    )


def mix(coup, scale, mass, u, d, k):
    out = []
    for c in range(3):
        a = (coup[c][0] * scale) * u[0]
        a = a + (coup[c][1] * scale) * u[1]
        a = a + (coup[c][2] * scale) * u[2]
        a = a + mass * d[c]
        out.append(k * a)
    return out


def flat_box(chunks, nz):
    rows = chunks[0].shape[0]
    lane = iota(chunks[0].shape, 1)
    zpos = lane & (nz - 1)
    s = []
    for v in chunks:
        v = v + pltpu.roll(v, 1, 0) + pltpu.roll(v, rows - 1, 0)
        s.append(
            v
            + jnp.where(zpos == 0, 0.0, pltpu.roll(v, 1, 1))
            + jnp.where(zpos == nz - 1, 0.0, pltpu.roll(v, 127, 1))
        )
    up = [pltpu.roll(v, nz, 1) for v in s]
    down = [pltpu.roll(v, 128 - nz, 1) for v in s]
    out = []
    for j, v in enumerate(s):
        before = up[j - 1] if j > 0 else 0.0
        after = down[j + 1] if j + 1 < len(s) else 0.0
        out.append(
            v
            + jnp.where(lane < nz, before, up[j])
            + jnp.where(lane >= 128 - nz, after, down[j])
        )
    return out


def flat_smooth(f, kappa, coup, level, nz, want_rest):
    theta, steps = chebyshev(level)
    scale = 4.0**-level / 26.0
    n = len(kappa)

    def apply(r, d):
        boxes = [flat_box(d[c], nz) for c in range(3)]
        new = [[None] * n for _ in range(3)]
        for j in range(n):
            u = [27.0 * d[c][j] - boxes[c][j] for c in range(3)]
            a = mix(coup, scale, MASS, u, [d[c][j] for c in range(3)], kappa[j])
            for c in range(3):
                new[c][j] = r[c][j] - a[c]
        return new

    r = f
    d = [[v * (1.0 / theta) for v in f[c]] for c in range(3)]
    x = d
    for a, b in steps:
        r = apply(r, d)
        d = [[a * d[c][j] + b * r[c][j] for j in range(n)] for c in range(3)]
        x = [[x[c][j] + d[c][j] for j in range(n)] for c in range(3)]
    if want_rest:
        r = apply(r, d)
    return x, r


def kernel(
    nw,
    nn,
    res,
    stiff,
    coup_ref,
    acc_out,
    tail_out,
    f0,
    k0,
    r0,
    d1,
    d2,
    d3,
    acc,
    t0,
    g1,
    r1,
    e1,
    w1,
    e2,
    w2,
    t1,
    u_lo,
    u_hi,
    g2,
    t2,
    v2,
    h3,
    h3s,
    t3,
    z4,
    m01,
    m12,
    m23,
    m34,
    p1,
    p2,
    p34,
    local_sem,
    s0,
    q0,
    s1,
    q1,
    s2,
    q2,
    s3,
    q3,
    s4,
    q4,
):
    w = lax.axis_index("wide")
    n = lax.axis_index("narrow")

    def there(ow, on):
        ok = None
        for pos, off, size in ((w, ow, nw), (n, on, nn)):
            if off > 0:
                c = pos + off < size
            elif off < 0:
                c = pos + off >= 0
            else:
                continue
            ok = c if ok is None else jnp.logical_and(ok, c)
        return ok

    def remote(src, dst, send, recv, ow, on):
        return pltpu.make_async_remote_copy(
            src_ref=src,
            dst_ref=dst,
            send_sem=send,
            recv_sem=recv,
            device_id={"wide": w + ow, "narrow": n + on},
            device_id_type=MESH,
        )

    own_f = pltpu.make_async_copy(res, f0.at[:, 4:20, 0:16, :], local_sem.at[0])
    own_k = pltpu.make_async_copy(stiff, k0.at[4:20, 0:16, :], local_sem.at[1])
    own_k.start()
    own_f.start()

    g1[...] = jnp.zeros_like(g1)
    g2[...] = jnp.zeros_like(g2)
    h3[...] = jnp.zeros_like(h3)
    h3s[...] = jnp.zeros_like(h3s)

    barrier = pltpu.get_barrier_semaphore()
    partners = NEIGHBOURS + [(o, 0) for o in WINDOW if abs(o) > 1]
    partners += [(0, o) for o in WINDOW if abs(o) > 1]
    count = 0
    for ow, on in partners:
        ok = there(ow, on)
        count = count + jnp.where(ok, 1, 0)

        @pl.when(ok)
        def _(ow=ow, on=on):
            pl.semaphore_signal(
                barrier,
                inc=1,
                device_id={"wide": w + ow, "narrow": n + on},
                device_id_type=MESH,
            )

    pl.semaphore_wait(barrier, count)

    def copies0(i, ow, on):
        sx, dx = {0: ((0, 16), (4, 20)), 1: ((12, 16), (0, 4)), -1: ((0, 4), (20, 24))}[ow]
        sy, dy = {0: ((0, 16), (0, 16)), 1: ((12, 16), (20, 24)), -1: ((0, 4), (16, 20))}[on]
        sx, dx, sy, dy = slice(*sx), slice(*dx), slice(*sy), slice(*dy)
        return (
            remote(res.at[:, sx, sy, :], f0.at[:, dx, dy, :], s0.at[i], q0.at[i], ow, on),
            remote(stiff.at[sx, sy, :], k0.at[dx, dy, :], s0.at[8 + i], q0.at[8 + i], ow, on),
        )

    def copies1(i, ow, on):
        sx, dx = {0: ((2, 6), (2, 6)), 1: ((4, 6), (0, 2)), -1: ((2, 4), (6, 8))}[ow]
        sy, dy = {0: ((0, 8), (0, 8)), 1: ((4, 8), (12, 16)), -1: ((0, 4), (8, 12))}[on]
        sx, dx, sy, dy = slice(*sx), slice(*dx), slice(*sy), slice(*dy)
        return (
            remote(g1.at[:, sx, sy, :], g1.at[:, dx, dy, :], s1.at[i], q1.at[i], ow, on),
        )

    def copies2(i, ow, on):
        dx = slice(4 - 4 * ow, 8 - 4 * ow)
        dy = slice(128 - 128 * on, 256 - 128 * on)
        return (
            remote(g2.at[:, 4:8, 128:256], g2.at[:, dx, dy], s2.at[i], q2.at[i], ow, on),
        )

    def copies3(i, ow, on):
        rows = slice(10 - 2 * ow, 12 - 2 * ow)
        return (remote(h3.at[10:12, :], h3.at[rows, :], s3.at[i], q3.at[i], ow, on),)

    def copies4(i, ow, on):
        return (remote(h3, h3s.at[5 - on], s4.at[i], q4.at[i], ow, on),)

    def start(copies, offsets, chosen=None):
        for i, (ow, on) in enumerate(offsets):
            if chosen is None or i in chosen:

                @pl.when(there(ow, on))
                def _(i=i, ow=ow, on=on):
                    for c in copies(i, ow, on):
                        c.start()

    def arrive(copies, offsets, chosen=None):
        for i, (ow, on) in enumerate(offsets):
            if chosen is None or i in chosen:

                @pl.when(there(-ow, -on))
                def _(i=i, ow=ow, on=on):
                    for c in copies(i, ow, on):
                        c.wait_recv()

    def sent(copies, offsets):
        for i, (ow, on) in enumerate(offsets):

            @pl.when(there(ow, on))
            def _(i=i, ow=ow, on=on):
                for c in copies(i, ow, on):
                    c.wait_send()

    along_wide = [(o, 0) for o in WINDOW]
    along_narrow = [(0, o) for o in WINDOW]

    start(copies0, NEIGHBOURS)

    @pl.when(w == 0)
    def _():
        f0[:, 0:4] = jnp.zeros((3, 4, 24, 128), F32)
        k0[0:4] = jnp.zeros((4, 24, 128), F32)

    @pl.when(w == nw - 1)
    def _():
        f0[:, 20:24] = jnp.zeros((3, 4, 24, 128), F32)
        k0[20:24] = jnp.zeros((4, 24, 128), F32)

    @pl.when(n == 0)
    def _():
        f0[:, :, 20:24, :] = jnp.zeros((3, 24, 4, 128), F32)
        k0[:, 20:24, :] = jnp.zeros((24, 4, 128), F32)

    @pl.when(n == nn - 1)
    def _():
        f0[:, :, 16:20, :] = jnp.zeros((3, 24, 4, 128), F32)
        k0[:, 16:20, :] = jnp.zeros((24, 4, 128), F32)

    r, c = iota((256, 128), 0), iota((256, 128), 1)
    m01[...] = indicator(((r >> 7) == (c >> 6)) & (((r & 127) >> 1) == (c & 63)), 0.125)
    r, c = iota((512, 128), 0), iota((512, 128), 1)
    m12[...] = indicator(((r >> 7) == (c >> 5)) & (((r & 63) >> 1) == (c & 31)), 0.125)
    m23[...] = indicator(
        ((r >> 7) == (c >> 5))
        & (((r >> 6) & 1) == ((c >> 4) & 1))
        & (((r & 31) >> 1) == (c & 15)),
        0.125,
    )
    r, c = iota((384, 128), 0), iota((384, 128), 1)
    m34[...] = indicator(((r >> 5) == (c >> 3)) & (((r & 15) >> 1) == (c & 7)), 0.125)
    r, c = iota((128, 256), 0), iota((128, 256), 1)
    p1[...] = indicator(((r >> 6) == (c >> 7)) & ((r & 63) == ((c & 127) >> 1)))
    r, c = iota((128, 512), 0), iota((128, 512), 1)
    p2[...] = indicator(((r >> 5) == (c >> 7)) & ((r & 31) == ((c & 127) >> 2)))
    r, c = iota((256, 256), 0), iota((256, 256), 1)
    fine = ((r >> 4) == (2 + (c >> 7))) & ((r & 15) == ((c & 127) >> 3))
    coarse = (r >= 128 + 40) & (r < 128 + 48) & ((r & 7) == ((c & 127) >> 4))
    p34[...] = indicator(fine | coarse)

    coup = [[coup_ref[i, j] for j in range(3)] for i in range(3)]

    own_k.wait()
    for i in range(8):
        t0[pl.ds(384 + 16 * i, 16), :] = (
            k0[4 + 2 * i, 0:16, :] + k0[5 + 2 * i, 0:16, :]
        )

    theta0, steps0 = chebyshev(0)
    lane24 = iota((24, 128), 1)

    def plane0(i, d, k_of, scale, mass):
        us, ds_ = [], []
        for c in range(3):
            mid = d[c, i]
            s = d[c, i - 1] + mid + d[c, i + 1]
            s = s + pltpu.roll(s, 1, 0) + pltpu.roll(s, 23, 0)
            s = (
                s
                + jnp.where(lane24 == 0, 0.0, pltpu.roll(s, 1, 1))
                + jnp.where(lane24 == 127, 0.0, pltpu.roll(s, 127, 1))
            )
            us.append(27.0 * mid - s)
            ds_.append(mid)
        return ds_, mix(coup, scale, mass, us, ds_, k_of[i])

    fields = [f0, d1, d2, d3]

    def sweep0(k, lo, pairs):
        d = fields[k]
        over = 1.0 / theta0 if k == 0 else 1.0
        scale, mass = over / 26.0, over * MASS
        rest = f0 if k == 0 else r0

        def body(t, carry):
            both = []
            for u in range(2):
                i = lo + 2 * t + u
                mids, a = plane0(i, d, k0, scale, mass)
                new = [rest[c, i] - a[c] for c in range(3)]
                if k < 3:
                    ca, cb = steps0[k]
                    for c in range(3):
                        r0[c, i] = new[c]
                        fields[k + 1][c, i] = (ca * over) * mids[c] + cb * new[c]
                both.append(new)
            if k == 3:
                half = (lo - 4) // 2 + t
                for c in range(3):
                    rows = pl.multiple_of(128 * c + 16 * half, 16)
                    t0[pl.ds(rows, 16), :] = both[0][c][0:16] + both[1][c][0:16]
            return carry

        lax.fori_loop(0, pairs, body, 0)

    own_f.wait()
    arrive(copies0, NEIGHBOURS, (2, 3))
    for k in range(4):
        sweep0(k, 5 + k, 7 - k) if k < 3 else sweep0(3, 8, 4)
    arrive(copies0, NEIGHBOURS, (0, 1, 4, 5, 6, 7))
    for k in range(4):
        sweep0(k, 1 + k, 2)
        sweep0(k, 19 - k, 2)

    s = t0[pl.ds(0, 256, stride=2), :] + t0[pl.ds(1, 256, stride=2), :]
    s = s.reshape(4, 4, 2, 8, 128)
    pair = jnp.concatenate(
        [s[:, :, 0].reshape(128, 128), s[:, :, 1].reshape(128, 128)], axis=1
    )
    g1[:, 2:6, 0:8, :] = mm(pair, m01[...]).reshape(4, 4, 8, 128)
    start(copies1, NEIGHBOURS)

    def sum0(i, carry):
        for c in range(3):
            acc[c, i] = (
                f0[c, 4 + i, 0:16, :] * (1.0 / theta0)
                + d1[c, 4 + i, 0:16, :]
                + d2[c, 4 + i, 0:16, :]
                + d3[c, 4 + i, 0:16, :]
            )
        return carry

    lax.fori_loop(0, 16, sum0, 0)

    arrive(copies1, NEIGHBOURS)

    theta1, steps1 = chebyshev(1)
    lane16 = iota((16, 128), 1)
    lower = lane16 < 64
    zpos1 = lane16 & 63
    for p in range(8):
        for c in range(3):
            w1[c, p] = pltpu.roll(g1[c, p], 64, 1)

    def plane1(p, d, wd, scale, mass):
        us, mids = [], []
        for c in range(3):
            mid = d[c, p]
            before = wd[c, max(p - 1, 0)]
            after = wd[c, min(p + 1, 7)]
            s = mid + wd[c, p] + jnp.where(lower, before, after)
            s = s + pltpu.roll(s, 1, 0) + pltpu.roll(s, 15, 0)
            s = (
                s
                + jnp.where(zpos1 == 0, 0.0, pltpu.roll(s, 1, 1))
                + jnp.where(zpos1 == 63, 0.0, pltpu.roll(s, 127, 1))
            )
            us.append(27.0 * mid - s)
            mids.append(mid)
        return mids, mix(coup, scale, mass, us, mids, g1[3, p])

    x1 = {}
    pairs1 = [(g1, w1), (e1, w2), (e2, w1), (e1, w2)]
    for k, (lo, hi) in enumerate([(0, 8), (1, 7), (1, 7), (2, 6)]):
        d, wd = pairs1[k]
        over = 1.0 / theta1 if k == 0 else 1.0
        scale, mass = over / (4.0 * 26.0), over * MASS
        for p in range(lo, hi):
            mids, a = plane1(p, d, wd, scale, mass)
            for c in range(3):
                new = (g1 if k == 0 else r1)[c, p] - a[c]
                if k < 3:
                    ca, cb = steps1[k]
                    nd, nwd = pairs1[k + 1]
                    r1[c, p] = new
                    step = (ca * over) * mids[c] + cb * new
                    nd[c, p] = step
                    nwd[c, p] = pltpu.roll(step, 64, 1)
                else:
                    t1[pl.ds(32 * c + 8 * (p - 2), 8), :] = new[0:8]
                if 2 <= p < 6:
                    part = (mids[c] * over)[0:8]
                    x1[c, p] = part if k == 0 else x1[c, p] + part
    for p in range(4):
        t1[pl.ds(96 + 8 * p, 8), :] = g1[3, 2 + p, 0:8, :]

    ys = [t1[pl.ds(y, 16, stride=8), :] for y in range(8)]
    ys = jnp.concatenate([ys[2 * j] + ys[2 * j + 1] for j in range(4)], axis=1)
    blk = mm(ys, m12[...])
    for c in range(4):
        g2[c, 4:8, 128:256] = blk[4 * c : 4 * c + 4]
    start(copies2, NEIGHBOURS)

    rows = jnp.concatenate([x1[c, p] for c in range(3) for p in range(2, 6)], axis=0)
    rep = mm(rows, p1[...])
    u_lo[pl.ds(0, 96, stride=2), :] = rep[:, 0:128]
    u_lo[pl.ds(1, 96, stride=2), :] = rep[:, 0:128]
    u_hi[pl.ds(0, 96, stride=2), :] = rep[:, 128:256]
    u_hi[pl.ds(1, 96, stride=2), :] = rep[:, 128:256]
    for c in range(3):
        for p in range(4):
            rows_cp = pl.ds(16 * (4 * c + p), 16)
            for j in range(4):
                acc[c, 4 * p + j] += (u_lo if j < 2 else u_hi)[rows_cp, :]

    arrive(copies2, NEIGHBOURS)
    f2 = [[g2[c, :, 128 * j : 128 * j + 128] for j in range(3)] for c in range(4)]
    x2, r2 = flat_smooth(f2[:3], f2[3], coup, 2, 32, True)

    t2[...] = mm(
        jnp.concatenate([r2[0][1], r2[1][1], r2[2][1], f2[3][1]], axis=1), m23[...]
    )
    h3[10:12, :] = t2[pl.ds(4, 2, stride=2), :] + t2[pl.ds(5, 2, stride=2), :]
    start(copies3, along_wide)

    for c in range(3):
        t3[4 * c : 4 * c + 4, 0:128] = x2[c][1][4:8]
    rep = mm(t3[0:16, 0:128], p2[...])
    for y in range(16):
        j = y // 4
        v2[pl.ds(y, 16, stride=16), :] = rep[:, 128 * j : 128 * j + 128]
    for c in range(3):
        for k in range(4):
            part = v2[pl.ds(16 * (4 * c + k), 16), :]
            for j in range(4):
                acc[c, 4 * k + j] += part
    whole = pltpu.make_async_copy(acc, acc_out, local_sem.at[2])
    whole.start()

    arrive(copies3, along_wide)
    start(copies4, along_narrow)
    arrive(copies4, along_narrow)

    lane3 = iota((24, 128), 1)
    slots = [h3s[j] if j != 5 else h3[...] for j in range(11)]
    f3 = [[None] * 3 for _ in range(4)]
    for c in range(4):
        for v in range(3):
            out = jnp.zeros((24, 128), F32)
            for q in range(4):
                j = 4 * v + q
                if j < 11:
                    turn = 32 * ((q - c) % 4)
                    part = pltpu.roll(slots[j], turn, 1) if turn else slots[j]
                    out = jnp.where((lane3 >> 5) == q, part, out)
            f3[c][v] = out
    x3, r3 = flat_smooth(f3[:3], f3[3], coup, 3, 16, True)

    for c in range(4):
        src = jnp.concatenate(r3[c] if c < 3 else f3[3], axis=1)
        t3[24 * c : 24 * c + 24, :] = src
    s = mm(t3[...], m34[...])
    z4[...] = s
    s = z4[pl.ds(0, 48, stride=2), :] + z4[pl.ds(1, 48, stride=2), :]
    pad = jnp.zeros((4, 128), F32)
    f4 = [[jnp.concatenate([s[12 * c : 12 * c + 12], pad], axis=0)] for c in range(4)]
    x4, _ = flat_smooth(f4[:3], f4[3], coup, 4, 8, False)

    for c in range(3):
        t3[2 * c : 2 * c + 2, 0:128] = x3[c][1][10:12]
        t3[2 * c : 2 * c + 2, 128:256] = jnp.broadcast_to(x4[c][0][5:6], (2, 128))
    tail_out[...] = mm(t3[0:16, 0:256], p34[...])[0:8]

    whole.wait()
    sent(copies0, NEIGHBOURS)
    sent(copies1, NEIGHBOURS)
    sent(copies2, NEIGHBOURS)
    sent(copies3, along_wide)
    sent(copies4, along_narrow)


def solution(mesh):
    nw, nn = mesh.shape["wide"], mesh.shape["narrow"]

    def vm(*shape):
        return pltpu.VMEM(shape, F32)

    def mat(*shape):
        return pltpu.VMEM(shape, BF16)

    dma = pltpu.SemaphoreType.DMA
    scratch = [
        vm(3, 24, 24, 128),
        vm(24, 24, 128),
        vm(3, 24, 24, 128),
        vm(3, 24, 24, 128),
        vm(3, 24, 24, 128),
        vm(3, 24, 24, 128),
        vm(3, 16, 16, 128),
        vm(512, 128),
        vm(4, 8, 16, 128),
        vm(3, 8, 16, 128),
        vm(3, 8, 16, 128),
        vm(3, 8, 16, 128),
        vm(3, 8, 16, 128),
        vm(3, 8, 16, 128),
        vm(128, 128),
        vm(192, 128),
        vm(192, 128),
        vm(4, 16, 384),
        vm(16, 128),
        vm(256, 128),
        vm(24, 128),
        vm(11, 24, 128),
        vm(96, 384),
        vm(96, 128),
        mat(256, 128),
        mat(512, 128),
        mat(512, 128),
        mat(384, 128),
        mat(128, 256),
        mat(128, 512),
        mat(256, 256),
        dma((3,)),
        dma((16,)),
        dma((16,)),
        dma((8,)),
        dma((8,)),
        dma((8,)),
        dma((8,)),
        dma((10,)),
        dma((10,)),
        dma((10,)),
        dma((10,)),
    ]

    def per_device(residual, stiffness, coupling):
        any_space = pl.BlockSpec(memory_space=pl.ANY)
        acc, tail = pl.pallas_call(
            functools.partial(kernel, nw, nn),
            out_shape=(
                jax.ShapeDtypeStruct((3, 16, 16, 128), F32),
                jax.ShapeDtypeStruct((8, 256), F32),
            ),
            in_specs=[any_space, any_space, pl.BlockSpec(memory_space=pltpu.SMEM)],
            out_specs=(any_space, pl.BlockSpec(memory_space=pltpu.VMEM)),
            scratch_shapes=scratch,
            compiler_params=pltpu.CompilerParams(
                collective_id=0,
                has_side_effects=True,
                vmem_limit_bytes=32 * 1024 * 1024,
            ),
        )(residual, stiffness, coupling)
        tail = tail[0:6].reshape(3, 2, 1, 2, 1, 128)
        return (acc.reshape(3, 2, 8, 2, 8, 128) + tail).reshape(3, 16, 16, 128)

    return jax.shard_map(
        per_device,
        mesh=mesh,
        in_specs=(P(None, "wide", "narrow", None), P("wide", "narrow", None), P()),
        out_specs=P(None, "wide", "narrow", None),
        check_vma=False,
    )
```

profile of v0, /device:TPU:1, one launch (start us, length us, event | category | flops | bytes accessed | tf_op | source)
XLA Modules:
  0.0 48.9 jit_solution(7920684264223626719)
XLA Ops:
  0.0 0.0 copy-start
  0.0 1.0 %copy-done = f32[3,16,16,128]{3,2,1,0:T(8,128)S(1)} copy-done((f32[3,16,16,128]{3,2,1,0:T(8,128)S(1)}, f32[3,16,16,128]{3,2,1,0:T(8,128)}, u32[]{:S(2)}) %copy-start) | copy-done | bytes 393240
  1.0 0.0 copy-start.1
  1.0 0.9 %copy-done.1 = f32[16,16,128]{2,1,0:T(8,128)S(1)} copy-done((f32[16,16,128]{2,1,0:T(8,128)S(1)}, f32[16,16,128]{2,1,0:T(8,128)}, u32[]{:S(2)}) %copy-start.1) | copy-done | bytes 131096
  1.9 0.0 copy-start.2
  1.9 0.7 %copy-done.2 = f32[3,3]{1,0:T(4,128)S(1)} copy-done((f32[3,3]{1,0:T(4,128)S(1)}, f32[3,3]{1,0:T(4,128)}, u32[]{:S(2)}) %copy-start.2) | copy-done | bytes 60
  2.6 45.5 %shard_map.37 = (f32[3,16,16,128]{3,2,1,0:T(8,128)S(1)}, f32[8,256]{1,0:T(8,128)S(1)}) custom-call(f32[3,16,16,128]{3,2,1,0:T(8,128)S(1)} %copy-done, f32[16,16,128]{2,1,0:T(8,128)S(1)} %copy-done.1, f32[3,3]{1,0:T(4,128)S(1)} %copy-done.2), custom_call_target="tpu_custom_call" | custom-call | tf_op jit(solution)/shard_map/pallas_call | solution.py:600
  48.1 0.8 %add.16 = f32[3,16,16,128]{3,2,1,0:T(8,128)} add(f32[3,16,16,128]{3,2,1,0:T(8,128)S(1)} %get-tuple-element.7, f32[3,16,16,128]{3,2,1,0:T(8,128)S(1)} %bitcast.3) | non-fusion elementwise | flops 98304 | bytes 1179648 | tf_op jit(solution)/shard_map/add | solution.py:616
  (2 shorter events, 0.0 us)
Async XLA Ops:
  0.0 1.0 %copy-start = (f32[3,16,16,128]{3,2,1,0:T(8,128)S(1)}, f32[3,16,16,128]{3,2,1,0:T(8,128)}, u32[]{:S(2)}) copy-start(f32[3,16,16,128]{3,2,1,0:T(8,128)} %res.1) | copy-start | bytes 1179652
  1.0 0.9 %copy-start.1 = (f32[16,16,128]{2,1,0:T(8,128)S(1)}, f32[16,16,128]{2,1,0:T(8,128)}, u32[]{:S(2)}) copy-start(f32[16,16,128]{2,1,0:T(8,128)} %stiff.1) | copy-start | bytes 393220
  1.9 0.7 %copy-start.2 = (f32[3,3]{1,0:T(4,128)S(1)}, f32[3,3]{1,0:T(4,128)}, u32[]{:S(2)}) copy-start(f32[3,3]{1,0:T(4,128)} %coup_ref.1) | copy-start | bytes 112
where the time goes:
time: 49.1 us; the launch traced here: 48.9 us
  Pallas kernels  45.5 us (93%)
  local copies, waits for them, and re-layouts  2.62 us (5%)
  other arithmetic  0.8 us (2%)
    pallas_call x1, Pallas kernels, per_device(): pl.pallas_call(functools.partial(kernel, nw, nn), out_shape=(jax.ShapeDty...  45.5 us
    unnamed x6, local copies, waits for them, and re-layouts  2.58 us

commit v1 on v0

--- a/solution.py
+++ b/solution.py
@@ -11,8 +11,8 @@
 MASS = 0.001
 RATIO = 8.0
 MESH = pl.DeviceIdType.MESH
-NEIGHBOURS = [(1, 0), (-1, 0), (0, 1), (0, -1), (1, 1), (1, -1), (-1, 1), (-1, -1)]
-WINDOW = [o for k in range(1, 6) for o in (k, -k)]
+NEIGHBOURS = [(1, 1), (1, -1), (-1, 1), (-1, -1), (1, 0), (-1, 0), (0, 1), (0, -1)]
+WINDOW = [o for k in range(5, 0, -1) for o in (k, -k)]
 F32 = jnp.float32
 BF16 = jnp.bfloat16
 
@@ -116,18 +116,17 @@
     nn,
     res,
     stiff,
-    coup_ref,
-    acc_out,
+    coup_hbm,
+    acc,
     tail_out,
-    f0,
-    k0,
+    f0b,
+    k0b,
     r0,
     d1,
     d2,
     d3,
-    acc,
     t0,
-    g1,
+    g1b,
     r1,
     e1,
     w1,
@@ -136,11 +135,11 @@
     t1,
     u_lo,
     u_hi,
-    g2,
+    g2b,
     t2,
     v2,
-    h3,
-    h3s,
+    h3b,
+    h3sb,
     t3,
     z4,
     m01,
@@ -150,6 +149,7 @@
     p1,
     p2,
     p34,
+    coup_ref,
     local_sem,
     s0,
     q0,
@@ -164,33 +164,77 @@
 ):
     w = lax.axis_index("wide")
     n = lax.axis_index("narrow")
-
-    def there(ow, on):
-        ok = None
-        for pos, off, size in ((w, ow, nw), (n, on, nn)):
-            if off > 0:
-                c = pos + off < size
-            elif off < 0:
-                c = pos + off >= 0
-            else:
-                continue
-            ok = c if ok is None else jnp.logical_and(ok, c)
-        return ok
-
-    def remote(src, dst, send, recv, ow, on):
+    f0, k0, g1, g2, h3, h3s = (b.at[0] for b in (f0b, k0b, g1b, g2b, h3b, h3sb))
+
+    def pair_of(i):
+        return i + 1 - 2 * lax.rem(i, 2)
+
+    def out_of(pos, off, size):
+        if off == 0:
+            return jnp.bool_(False)
+        return pos + off >= size if off > 0 else pos + off < 0
+
+    targets = {}
+
+    def target(ow, on):
+        if (ow, on) in targets:
+            return targets[ow, on]
+        w_out, n_out = out_of(w, ow, nw), out_of(n, on, nn)
+        if on == 0:
+            tw = jnp.where(w_out, w, w + ow)
+            tn = jnp.where(w_out, pair_of(n), n)
+            away = w_out
+        elif ow == 0:
+            tw = jnp.where(n_out, pair_of(w), w)
+            tn = jnp.where(n_out, n, n + on)
+            away = n_out
+        else:
+            w_end, n_end = (nw - 1 if ow > 0 else 0), (nn - 1 if on > 0 else 0)
+            both = jnp.logical_and(w_out, n_out)
+            away = jnp.logical_or(w_out, n_out)
+            w_near, n_near = w == w_end - ow, n == n_end - on
+            tw = jnp.where(
+                both,
+                w - ow,
+                jnp.where(
+                    w_out,
+                    w,
+                    jnp.where(n_out, jnp.where(w_near, w + ow, pair_of(w)), w + ow),
+                ),
+            )
+            tn = jnp.where(
+                both,
+                n,
+                jnp.where(
+                    w_out,
+                    jnp.where(n_near, n + on, pair_of(n)),
+                    jnp.where(n_out, jnp.where(w_near, n - on, n), n + on),
+                ),
+            )
+        targets[ow, on] = tw, tn, jnp.where(away, 1, 0)
+        return targets[ow, on]
+
+    def remote(src, dst, where, send, recv, sems, ow, on):
+        tw, tn, away = target(ow, on)
+        mine, other = sems
         return pltpu.make_async_remote_copy(
             src_ref=src,
-            dst_ref=dst,
-            send_sem=send,
-            recv_sem=recv,
-            device_id={"wide": w + ow, "narrow": n + on},
+            dst_ref=dst.at[(away,) + where],
+            send_sem=send.at[mine],
+            recv_sem=recv.at[mine + (other - mine) * away],
+            device_id={"wide": tw, "narrow": tn},
             device_id_type=MESH,
         )
 
-    own_f = pltpu.make_async_copy(res, f0.at[:, 4:20, 0:16, :], local_sem.at[0])
-    own_k = pltpu.make_async_copy(stiff, k0.at[4:20, 0:16, :], local_sem.at[1])
-    own_k.start()
-    own_f.start()
+    def landed(buf, where, send, recv, mine):
+        return pltpu.make_async_remote_copy(
+            src_ref=buf.at[(0,) + where],
+            dst_ref=buf.at[(0,) + where],
+            send_sem=send.at[mine],
+            recv_sem=recv.at[mine],
+            device_id={"wide": w, "narrow": n},
+            device_id_type=MESH,
+        )
 
     g1[...] = jnp.zeros_like(g1)
     g2[...] = jnp.zeros_like(g2)
@@ -198,80 +242,78 @@
     h3s[...] = jnp.zeros_like(h3s)
 
     barrier = pltpu.get_barrier_semaphore()
-    partners = NEIGHBOURS + [(o, 0) for o in WINDOW if abs(o) > 1]
-    partners += [(0, o) for o in WINDOW if abs(o) > 1]
-    count = 0
-    for ow, on in partners:
-        ok = there(ow, on)
-        count = count + jnp.where(ok, 1, 0)
-
-        @pl.when(ok)
-        def _(ow=ow, on=on):
-            pl.semaphore_signal(
-                barrier,
-                inc=1,
-                device_id={"wide": w + ow, "narrow": n + on},
-                device_id_type=MESH,
-            )
-
-    pl.semaphore_wait(barrier, count)
+    near = NEIGHBOURS + [(2, 0), (-2, 0), (0, 2), (0, -2)]
+    for ow, on in near:
+        tw, tn, _ = target(ow, on)
+        pl.semaphore_signal(
+            barrier,
+            inc=1,
+            device_id={"wide": tw, "narrow": tn},
+            device_id_type=MESH,
+        )
+
+    own_f = pltpu.make_async_copy(res, f0.at[:, 4:20, 0:16, :], local_sem.at[0])
+    own_k = pltpu.make_async_copy(stiff, k0.at[4:20, 0:16, :], local_sem.at[1])
+    own_c = pltpu.make_async_copy(coup_hbm, coup_ref, local_sem.at[2])
+    own_k.start()
+    own_f.start()
+    own_c.start()
+
+    pl.semaphore_wait(barrier, len(near))
 
     def copies0(i, ow, on):
-        sx, dx = {0: ((0, 16), (4, 20)), 1: ((12, 16), (0, 4)), -1: ((0, 4), (20, 24))}[ow]
-        sy, dy = {0: ((0, 16), (0, 16)), 1: ((12, 16), (20, 24)), -1: ((0, 4), (16, 20))}[on]
-        sx, dx, sy, dy = slice(*sx), slice(*dx), slice(*sy), slice(*dy)
-        return (
-            remote(res.at[:, sx, sy, :], f0.at[:, dx, dy, :], s0.at[i], q0.at[i], ow, on),
-            remote(stiff.at[sx, sy, :], k0.at[dx, dy, :], s0.at[8 + i], q0.at[8 + i], ow, on),
-        )
+        sx, dx = {0: (0, 4), 1: (12, 0), -1: (0, 20)}[ow]
+        sy, dy = {0: (0, 0), 1: (12, 20), -1: (0, 16)}[on]
+        nx, ny = (16 if ow == 0 else 4), (16 if on == 0 else 4)
+        fs = (slice(None), slice(sx, sx + nx), slice(sy, sy + ny))
+        fd = (slice(None), slice(dx, dx + nx), slice(dy, dy + ny))
+        if ow > 0:
+            sx, dx = sx + 1, dx + 1
+        if on > 0:
+            sy, dy = sy + 1, dy + 1
+        nx, ny = (16 if ow == 0 else 3), (16 if on == 0 else 3)
+        ks = (slice(sx, sx + nx), slice(sy, sy + ny))
+        kd = (slice(dx, dx + nx), slice(dy, dy + ny))
+        return [
+            (res.at[fs], f0b, fd, s0, q0, i),
+            (stiff.at[ks], k0b, kd, s0, q0, 8 + i),
+        ]
 
     def copies1(i, ow, on):
         sx, dx = {0: ((2, 6), (2, 6)), 1: ((4, 6), (0, 2)), -1: ((2, 4), (6, 8))}[ow]
         sy, dy = {0: ((0, 8), (0, 8)), 1: ((4, 8), (12, 16)), -1: ((0, 4), (8, 12))}[on]
-        sx, dx, sy, dy = slice(*sx), slice(*dx), slice(*sy), slice(*dy)
-        return (
-            remote(g1.at[:, sx, sy, :], g1.at[:, dx, dy, :], s1.at[i], q1.at[i], ow, on),
-        )
+        src = g1.at[:, slice(*sx), slice(*sy), :]
+        return [(src, g1b, (slice(None), slice(*dx), slice(*dy)), s1, q1, i)]
 
     def copies2(i, ow, on):
         dx = slice(4 - 4 * ow, 8 - 4 * ow)
         dy = slice(128 - 128 * on, 256 - 128 * on)
-        return (
-            remote(g2.at[:, 4:8, 128:256], g2.at[:, dx, dy], s2.at[i], q2.at[i], ow, on),
-        )
+        return [(g2.at[:, 4:8, 128:256], g2b, (slice(None), dx, dy), s2, q2, i)]
 
     def copies3(i, ow, on):
         rows = slice(10 - 2 * ow, 12 - 2 * ow)
-        return (remote(h3.at[10:12, :], h3.at[rows, :], s3.at[i], q3.at[i], ow, on),)
+        return [(h3.at[10:12, :], h3b, (rows,), s3, q3, i)]
 
     def copies4(i, ow, on):
-        return (remote(h3, h3s.at[5 - on], s4.at[i], q4.at[i], ow, on),)
-
-    def start(copies, offsets, chosen=None):
+        return [(h3, h3sb, (5 - on,), s4, q4, i)]
+
+    def start(copies, offsets):
         for i, (ow, on) in enumerate(offsets):
-            if chosen is None or i in chosen:
-
-                @pl.when(there(ow, on))
-                def _(i=i, ow=ow, on=on):
-                    for c in copies(i, ow, on):
-                        c.start()
+            opposite = offsets.index((-ow, -on))
+            for src, dst, where, send, recv, mine in copies(i, ow, on):
+                sems = mine, mine + opposite - i
+                remote(src, dst, where, send, recv, sems, ow, on).start()
 
     def arrive(copies, offsets, chosen=None):
         for i, (ow, on) in enumerate(offsets):
             if chosen is None or i in chosen:
-
-                @pl.when(there(-ow, -on))
-                def _(i=i, ow=ow, on=on):
-                    for c in copies(i, ow, on):
-                        c.wait_recv()
+                for src, dst, where, send, recv, mine in copies(i, ow, on):
+                    landed(dst, where, send, recv, mine).wait_recv()
 
     def sent(copies, offsets):
         for i, (ow, on) in enumerate(offsets):
-
-            @pl.when(there(ow, on))
-            def _(i=i, ow=ow, on=on):
-                for c in copies(i, ow, on):
-                    c.wait_send()
+            for src, dst, where, send, recv, mine in copies(i, ow, on):
+                landed(dst, where, send, recv, mine).wait_send()
 
     along_wide = [(o, 0) for o in WINDOW]
     along_narrow = [(0, o) for o in WINDOW]
@@ -319,6 +361,7 @@
     coarse = (r >= 128 + 40) & (r < 128 + 48) & ((r & 7) == ((c & 127) >> 4))
     p34[...] = indicator(fine | coarse)
 
+    own_c.wait()
     coup = [[coup_ref[i, j] for j in range(3)] for i in range(3)]
 
     own_k.wait()
@@ -375,10 +418,10 @@
         lax.fori_loop(0, pairs, body, 0)
 
     own_f.wait()
-    arrive(copies0, NEIGHBOURS, (2, 3))
+    arrive(copies0, NEIGHBOURS, (6, 7))
     for k in range(4):
         sweep0(k, 5 + k, 7 - k) if k < 3 else sweep0(3, 8, 4)
-    arrive(copies0, NEIGHBOURS, (0, 1, 4, 5, 6, 7))
+    arrive(copies0, NEIGHBOURS, (0, 1, 2, 3, 4, 5))
     for k in range(4):
         sweep0(k, 1 + k, 2)
         sweep0(k, 19 - k, 2)
@@ -390,6 +433,7 @@
     )
     g1[:, 2:6, 0:8, :] = mm(pair, m01[...]).reshape(4, 4, 8, 128)
     start(copies1, NEIGHBOURS)
+    sent(copies0, NEIGHBOURS)
 
     def sum0(i, carry):
         for c in range(3):
@@ -461,6 +505,7 @@
     for c in range(4):
         g2[c, 4:8, 128:256] = blk[4 * c : 4 * c + 4]
     start(copies2, NEIGHBOURS)
+    sent(copies1, NEIGHBOURS)
 
     rows = jnp.concatenate([x1[c, p] for c in range(3) for p in range(2, 6)], axis=0)
     rep = mm(rows, p1[...])
@@ -475,6 +520,7 @@
                 acc[c, 4 * p + j] += (u_lo if j < 2 else u_hi)[rows_cp, :]
 
     arrive(copies2, NEIGHBOURS)
+
     f2 = [[g2[c, :, 128 * j : 128 * j + 128] for j in range(3)] for c in range(4)]
     x2, r2 = flat_smooth(f2[:3], f2[3], coup, 2, 32, True)
 
@@ -483,6 +529,7 @@
     )
     h3[10:12, :] = t2[pl.ds(4, 2, stride=2), :] + t2[pl.ds(5, 2, stride=2), :]
     start(copies3, along_wide)
+    sent(copies2, NEIGHBOURS)
 
     for c in range(3):
         t3[4 * c : 4 * c + 4, 0:128] = x2[c][1][4:8]
@@ -495,12 +542,12 @@
             part = v2[pl.ds(16 * (4 * c + k), 16), :]
             for j in range(4):
                 acc[c, 4 * k + j] += part
-    whole = pltpu.make_async_copy(acc, acc_out, local_sem.at[2])
-    whole.start()
 
     arrive(copies3, along_wide)
     start(copies4, along_narrow)
+    sent(copies3, along_wide)
     arrive(copies4, along_narrow)
+    sent(copies4, along_narrow)
 
     lane3 = iota((24, 128), 1)
     slots = [h3s[j] if j != 5 else h3[...] for j in range(11)]
@@ -532,13 +579,6 @@
         t3[2 * c : 2 * c + 2, 128:256] = jnp.broadcast_to(x4[c][0][5:6], (2, 128))
     tail_out[...] = mm(t3[0:16, 0:256], p34[...])[0:8]
 
-    whole.wait()
-    sent(copies0, NEIGHBOURS)
-    sent(copies1, NEIGHBOURS)
-    sent(copies2, NEIGHBOURS)
-    sent(copies3, along_wide)
-    sent(copies4, along_narrow)
-
 
 def solution(mesh):
     nw, nn = mesh.shape["wide"], mesh.shape["narrow"]
@@ -551,15 +591,14 @@
 
     dma = pltpu.SemaphoreType.DMA
     scratch = [
-        vm(3, 24, 24, 128),
-        vm(24, 24, 128),
+        vm(2, 3, 24, 24, 128),
+        vm(2, 24, 24, 128),
         vm(3, 24, 24, 128),
         vm(3, 24, 24, 128),
         vm(3, 24, 24, 128),
         vm(3, 24, 24, 128),
-        vm(3, 16, 16, 128),
         vm(512, 128),
-        vm(4, 8, 16, 128),
+        vm(2, 4, 8, 16, 128),
         vm(3, 8, 16, 128),
         vm(3, 8, 16, 128),
         vm(3, 8, 16, 128),
@@ -568,11 +607,11 @@
         vm(128, 128),
         vm(192, 128),
         vm(192, 128),
-        vm(4, 16, 384),
+        vm(2, 4, 16, 384),
         vm(16, 128),
         vm(256, 128),
-        vm(24, 128),
-        vm(11, 24, 128),
+        vm(2, 24, 128),
+        vm(2, 11, 24, 128),
         vm(96, 384),
         vm(96, 128),
         mat(256, 128),
@@ -582,6 +621,7 @@
         mat(128, 256),
         mat(128, 512),
         mat(256, 256),
+        pltpu.SMEM((3, 3), F32),
         dma((3,)),
         dma((16,)),
         dma((16,)),
@@ -596,20 +636,21 @@
     ]
 
     def per_device(residual, stiffness, coupling):
-        any_space = pl.BlockSpec(memory_space=pl.ANY)
+        hbm = pl.BlockSpec(memory_space=pltpu.HBM)
+        vmem = pl.BlockSpec(memory_space=pltpu.VMEM)
         acc, tail = pl.pallas_call(
             functools.partial(kernel, nw, nn),
             out_shape=(
                 jax.ShapeDtypeStruct((3, 16, 16, 128), F32),
                 jax.ShapeDtypeStruct((8, 256), F32),
             ),
-            in_specs=[any_space, any_space, pl.BlockSpec(memory_space=pltpu.SMEM)],
-            out_specs=(any_space, pl.BlockSpec(memory_space=pltpu.VMEM)),
+            in_specs=[hbm, hbm, hbm],
+            out_specs=(vmem, vmem),
             scratch_shapes=scratch,
             compiler_params=pltpu.CompilerParams(
                 collective_id=0,
                 has_side_effects=True,
-                vmem_limit_bytes=32 * 1024 * 1024,
+                vmem_limit_bytes=(53 * 1024 + 300) * 1024,
             ),
         )(residual, stiffness, coupling)
         tail = tail[0:6].reshape(3, 2, 1, 2, 1, 128)

time: 49.1 us -> 45.1 us (0.919)
  Pallas kernels: 45.5 us -> 42.5 us
  local copies, waits for them, and re-layouts: 2.62 us -> 1.62 us
    pallas_call x1, Pallas kernels: 45.5 us -> 42.5 us  [per_device(): pl.pallas_call(functools.partial(kernel, nw, nn), out_shape=(jax.ShapeDty...]
    unnamed x6 -> x4, local copies, waits for them, and re-layouts: 2.58 us -> 1.58 us
where the time goes in v1:
time: 45.1 us; the launch traced here: 45 us
  Pallas kernels  42.5 us (94%)
  local copies, waits for them, and re-layouts  1.62 us (4%)
  other arithmetic  0.8 us (2%)
    pallas_call x1, Pallas kernels, per_device(): pl.pallas_call(functools.partial(kernel, nw, nn), out_shape=(jax.ShapeDty...  42.5 us
    unnamed x4, local copies, waits for them, and re-layouts  1.58 us

profile of v1, /device:TPU:1, one launch (start us, length us, event | category | flops | bytes accessed | tf_op | source)
XLA Modules:
  0.0 45.0 jit_solution(18067870955437558541)
XLA Ops:
  0.0 0.0 copy-start
  0.0 0.9 %copy-done = f32[16,16,128]{2,1,0:T(8,128)S(1)} copy-done((f32[16,16,128]{2,1,0:T(8,128)S(1)}, f32[16,16,128]{2,1,0:T(8,128)}, u32[]{:S(2)}) %copy-start) | copy-done | bytes 131096
  0.9 0.0 copy-start.1
  0.9 0.7 %copy-done.1 = f32[3,3]{1,0:T(4,128)S(1)} copy-done((f32[3,3]{1,0:T(4,128)S(1)}, f32[3,3]{1,0:T(4,128)}, u32[]{:S(2)}) %copy-start.1) | copy-done | bytes 60
  1.6 42.5 %shard_map.37 = (f32[3,16,16,128]{3,2,1,0:T(8,128)S(1)}, f32[8,256]{1,0:T(8,128)S(1)}) custom-call(f32[3,16,16,128]{3,2,1,0:T(8,128)} %res.1, f32[16,16,128]{2,1,0:T(8,128)S(1)} %copy-done, f32[3,3]{1,0:T(4,128)S(1)} %copy-done.1), custom_call_target="tpu_custom_call" | custom-call | tf_op jit(solution)/shard_map/pallas_call | solution.py:641
  44.2 0.8 %add.16 = f32[3,16,16,128]{3,2,1,0:T(8,128)} add(f32[3,16,16,128]{3,2,1,0:T(8,128)S(1)} %get-tuple-element.7, f32[3,16,16,128]{3,2,1,0:T(8,128)S(1)} %bitcast.3) | non-fusion elementwise | flops 98304 | bytes 1179648 | tf_op jit(solution)/shard_map/add | solution.py:657
  (2 shorter events, 0.0 us)
Async XLA Ops:
  0.0 0.9 %copy-start = (f32[16,16,128]{2,1,0:T(8,128)S(1)}, f32[16,16,128]{2,1,0:T(8,128)}, u32[]{:S(2)}) copy-start(f32[16,16,128]{2,1,0:T(8,128)} %stiff.1) | copy-start | bytes 393220
  0.9 0.7 %copy-start.1 = (f32[3,3]{1,0:T(4,128)S(1)}, f32[3,3]{1,0:T(4,128)}, u32[]{:S(2)}) copy-start(f32[3,3]{1,0:T(4,128)} %coup_hbm.1) | copy-start | bytes 112

commit v2 on v1

--- a/solution.py
+++ b/solution.py
@@ -12,6 +12,7 @@
 RATIO = 8.0
 MESH = pl.DeviceIdType.MESH
 NEIGHBOURS = [(1, 1), (1, -1), (-1, 1), (-1, -1), (1, 0), (-1, 0), (0, 1), (0, -1)]
+AXIAL = NEIGHBOURS[4:]
 WINDOW = [o for k in range(5, 0, -1) for o in (k, -k)]
 F32 = jnp.float32
 BF16 = jnp.bfloat16
@@ -117,7 +118,9 @@
     res,
     stiff,
     coup_hbm,
-    acc,
+    acc0,
+    acc1,
+    acc2,
     tail_out,
     f0b,
     k0b,
@@ -151,6 +154,7 @@
     p34,
     coup_ref,
     local_sem,
+    ready_sem,
     s0,
     q0,
     s1,
@@ -164,6 +168,7 @@
 ):
     w = lax.axis_index("wide")
     n = lax.axis_index("narrow")
+    acc = [acc0, acc1, acc2]
     f0, k0, g1, g2, h3, h3s = (b.at[0] for b in (f0b, k0b, g1b, g2b, h3b, h3sb))
 
     def pair_of(i):
@@ -236,47 +241,50 @@
             device_id_type=MESH,
         )
 
-    g1[...] = jnp.zeros_like(g1)
-    g2[...] = jnp.zeros_like(g2)
-    h3[...] = jnp.zeros_like(h3)
-    h3s[...] = jnp.zeros_like(h3s)
-
-    barrier = pltpu.get_barrier_semaphore()
-    near = NEIGHBOURS + [(2, 0), (-2, 0), (0, 2), (0, -2)]
-    for ow, on in near:
-        tw, tn, _ = target(ow, on)
-        pl.semaphore_signal(
-            barrier,
-            inc=1,
-            device_id={"wide": tw, "narrow": tn},
-            device_id_type=MESH,
-        )
-
     own_f = pltpu.make_async_copy(res, f0.at[:, 4:20, 0:16, :], local_sem.at[0])
     own_k = pltpu.make_async_copy(stiff, k0.at[4:20, 0:16, :], local_sem.at[1])
     own_c = pltpu.make_async_copy(coup_hbm, coup_ref, local_sem.at[2])
+    own_f.start()
     own_k.start()
-    own_f.start()
     own_c.start()
 
-    pl.semaphore_wait(barrier, len(near))
+    h3[...] = jnp.zeros_like(h3)
+    h3s[...] = jnp.zeros_like(h3s)
+
+    def tell(sem, offsets):
+        for ow, on in offsets:
+            tw, tn, _ = target(ow, on)
+            pl.semaphore_signal(
+                sem,
+                inc=1,
+                device_id={"wide": tw, "narrow": tn},
+                device_id_type=MESH,
+            )
+
+    barrier = pltpu.get_barrier_semaphore()
+    tell(barrier, AXIAL)
+    g1[...] = jnp.zeros_like(g1)
+    g2[...] = jnp.zeros_like(g2)
+    own_f.wait()
+    own_k.wait()
+    pl.semaphore_wait(barrier, len(AXIAL))
 
     def copies0(i, ow, on):
         sx, dx = {0: (0, 4), 1: (12, 0), -1: (0, 20)}[ow]
         sy, dy = {0: (0, 0), 1: (12, 20), -1: (0, 16)}[on]
         nx, ny = (16 if ow == 0 else 4), (16 if on == 0 else 4)
-        fs = (slice(None), slice(sx, sx + nx), slice(sy, sy + ny))
+        fs = (slice(None), slice(4 + sx, 4 + sx + nx), slice(sy, sy + ny))
         fd = (slice(None), slice(dx, dx + nx), slice(dy, dy + ny))
         if ow > 0:
             sx, dx = sx + 1, dx + 1
         if on > 0:
             sy, dy = sy + 1, dy + 1
         nx, ny = (16 if ow == 0 else 3), (16 if on == 0 else 3)
-        ks = (slice(sx, sx + nx), slice(sy, sy + ny))
+        ks = (slice(4 + sx, 4 + sx + nx), slice(sy, sy + ny))
         kd = (slice(dx, dx + nx), slice(dy, dy + ny))
         return [
-            (res.at[fs], f0b, fd, s0, q0, i),
-            (stiff.at[ks], k0b, kd, s0, q0, 8 + i),
+            (f0.at[fs], f0b, fd, s0, q0, i),
+            (k0.at[ks], k0b, kd, s0, q0, 8 + i),
         ]
 
     def copies1(i, ow, on):
@@ -297,12 +305,13 @@
     def copies4(i, ow, on):
         return [(h3, h3sb, (5 - on,), s4, q4, i)]
 
-    def start(copies, offsets):
+    def start(copies, offsets, chosen=None, part=slice(None)):
         for i, (ow, on) in enumerate(offsets):
-            opposite = offsets.index((-ow, -on))
-            for src, dst, where, send, recv, mine in copies(i, ow, on):
-                sems = mine, mine + opposite - i
-                remote(src, dst, where, send, recv, sems, ow, on).start()
+            if chosen is None or i in chosen:
+                opposite = offsets.index((-ow, -on))
+                for src, dst, where, send, recv, mine in copies(i, ow, on)[part]:
+                    sems = mine, mine + opposite - i
+                    remote(src, dst, where, send, recv, sems, ow, on).start()
 
     def arrive(copies, offsets, chosen=None):
         for i, (ow, on) in enumerate(offsets):
@@ -318,7 +327,12 @@
     along_wide = [(o, 0) for o in WINDOW]
     along_narrow = [(0, o) for o in WINDOW]
 
-    start(copies0, NEIGHBOURS)
+    start(copies0, NEIGHBOURS, (4, 5), slice(0, 1))
+    start(copies0, NEIGHBOURS, (6, 7))
+    tell(ready_sem, AXIAL)
+    pl.semaphore_wait(ready_sem, len(AXIAL))
+    start(copies0, NEIGHBOURS, (0, 1, 2, 3))
+    start(copies0, NEIGHBOURS, (4, 5), slice(1, 2))
 
     @pl.when(w == 0)
     def _():
@@ -364,7 +378,6 @@
     own_c.wait()
     coup = [[coup_ref[i, j] for j in range(3)] for i in range(3)]
 
-    own_k.wait()
     for i in range(8):
         t0[pl.ds(384 + 16 * i, 16), :] = (
             k0[4 + 2 * i, 0:16, :] + k0[5 + 2 * i, 0:16, :]
@@ -372,60 +385,52 @@
 
     theta0, steps0 = chebyshev(0)
     lane24 = iota((24, 128), 1)
-
-    def plane0(i, d, k_of, scale, mass):
-        us, ds_ = [], []
-        for c in range(3):
-            mid = d[c, i]
-            s = d[c, i - 1] + mid + d[c, i + 1]
-            s = s + pltpu.roll(s, 1, 0) + pltpu.roll(s, 23, 0)
-            s = (
-                s
-                + jnp.where(lane24 == 0, 0.0, pltpu.roll(s, 1, 1))
-                + jnp.where(lane24 == 127, 0.0, pltpu.roll(s, 127, 1))
-            )
-            us.append(27.0 * mid - s)
-            ds_.append(mid)
-        return ds_, mix(coup, scale, mass, us, ds_, k_of[i])
-
+    lane16 = iota((16, 128), 1)
     fields = [f0, d1, d2, d3]
 
-    def sweep0(k, lo, pairs):
+    def sweep0(k, starts, count):
         d = fields[k]
         over = 1.0 / theta0 if k == 0 else 1.0
         scale, mass = over / 26.0, over * MASS
         rest = f0 if k == 0 else r0
-
-        def body(t, carry):
-            both = []
-            for u in range(2):
-                i = lo + 2 * t + u
-                mids, a = plane0(i, d, k0, scale, mass)
-                new = [rest[c, i] - a[c] for c in range(3)]
-                if k < 3:
-                    ca, cb = steps0[k]
+        rows, lane = (24, lane24) if k < 3 else (16, lane16)
+        for lo in starts:
+            for i in range(lo, lo + count, 2):
+                mids, boxes = [[], []], [[], []]
+                for c in range(3):
+                    a, b = d[c, i], d[c, i + 1]
+                    both = a + b
+                    for u, (mid, x) in enumerate(((a, d[c, i - 1]), (b, d[c, i + 2]))):
+                        s = both + x
+                        s = s + pltpu.roll(s, 1, 0) + pltpu.roll(s, 23, 0)
+                        s = s[0:rows]
+                        s = (
+                            s
+                            + jnp.where(lane == 0, 0.0, pltpu.roll(s, 1, 1))
+                            + jnp.where(lane == 127, 0.0, pltpu.roll(s, 127, 1))
+                        )
+                        mids[u].append(mid[0:rows])
+                        boxes[u].append(s)
+                new = []
+                for u in range(2):
+                    us = [27.0 * mids[u][c] - boxes[u][c] for c in range(3)]
+                    a = mix(coup, scale, mass, us, mids[u], k0[i + u, 0:rows])
+                    new.append([rest[c, i + u, 0:rows] - a[c] for c in range(3)])
+                    if k < 3:
+                        ca, cb = steps0[k]
+                        for c in range(3):
+                            r0[c, i + u] = new[u][c]
+                            fields[k + 1][c, i + u] = (ca * over) * mids[u][c] + cb * new[u][c]
+                if k == 3:
                     for c in range(3):
-                        r0[c, i] = new[c]
-                        fields[k + 1][c, i] = (ca * over) * mids[c] + cb * new[c]
-                both.append(new)
-            if k == 3:
-                half = (lo - 4) // 2 + t
-                for c in range(3):
-                    rows = pl.multiple_of(128 * c + 16 * half, 16)
-                    t0[pl.ds(rows, 16), :] = both[0][c][0:16] + both[1][c][0:16]
-            return carry
-
-        lax.fori_loop(0, pairs, body, 0)
-
-    own_f.wait()
+                        t0[pl.ds(128 * c + 8 * (i - 4), 16), :] = new[0][c] + new[1][c]
+
     arrive(copies0, NEIGHBOURS, (6, 7))
     for k in range(4):
-        sweep0(k, 5 + k, 7 - k) if k < 3 else sweep0(3, 8, 4)
+        sweep0(k, (5 + k,), 14 - 2 * k)
     arrive(copies0, NEIGHBOURS, (0, 1, 2, 3, 4, 5))
     for k in range(4):
-        sweep0(k, 1 + k, 2)
-        sweep0(k, 19 - k, 2)
-
+        sweep0(k, (1 + k, 19 - k), 4)
     s = t0[pl.ds(0, 256, stride=2), :] + t0[pl.ds(1, 256, stride=2), :]
     s = s.reshape(4, 4, 2, 8, 128)
     pair = jnp.concatenate(
@@ -437,7 +442,7 @@
 
     def sum0(i, carry):
         for c in range(3):
-            acc[c, i] = (
+            acc[c][i] = (
                 f0[c, 4 + i, 0:16, :] * (1.0 / theta0)
                 + d1[c, 4 + i, 0:16, :]
                 + d2[c, 4 + i, 0:16, :]
@@ -450,7 +455,6 @@
     arrive(copies1, NEIGHBOURS)
 
     theta1, steps1 = chebyshev(1)
-    lane16 = iota((16, 128), 1)
     lower = lane16 < 64
     zpos1 = lane16 & 63
     for p in range(8):
@@ -517,7 +521,7 @@
         for p in range(4):
             rows_cp = pl.ds(16 * (4 * c + p), 16)
             for j in range(4):
-                acc[c, 4 * p + j] += (u_lo if j < 2 else u_hi)[rows_cp, :]
+                acc[c][4 * p + j] += (u_lo if j < 2 else u_hi)[rows_cp, :]
 
     arrive(copies2, NEIGHBOURS)
 
@@ -541,7 +545,7 @@
         for k in range(4):
             part = v2[pl.ds(16 * (4 * c + k), 16), :]
             for j in range(4):
-                acc[c, 4 * k + j] += part
+                acc[c][4 * k + j] += part
 
     arrive(copies3, along_wide)
     start(copies4, along_narrow)
@@ -623,6 +627,7 @@
         mat(256, 256),
         pltpu.SMEM((3, 3), F32),
         dma((3,)),
+        pltpu.SemaphoreType.REGULAR,
         dma((16,)),
         dma((16,)),
         dma((8,)),
@@ -638,23 +643,23 @@
     def per_device(residual, stiffness, coupling):
         hbm = pl.BlockSpec(memory_space=pltpu.HBM)
         vmem = pl.BlockSpec(memory_space=pltpu.VMEM)
-        acc, tail = pl.pallas_call(
+        *acc, tail = pl.pallas_call(
             functools.partial(kernel, nw, nn),
             out_shape=(
-                jax.ShapeDtypeStruct((3, 16, 16, 128), F32),
+                *[jax.ShapeDtypeStruct((16, 16, 128), F32)] * 3,
                 jax.ShapeDtypeStruct((8, 256), F32),
             ),
             in_specs=[hbm, hbm, hbm],
-            out_specs=(vmem, vmem),
+            out_specs=(vmem,) * 4,
             scratch_shapes=scratch,
             compiler_params=pltpu.CompilerParams(
                 collective_id=0,
                 has_side_effects=True,
-                vmem_limit_bytes=(53 * 1024 + 300) * 1024,
+                vmem_limit_bytes=(53 * 1024 + 450) * 1024,
             ),
         )(residual, stiffness, coupling)
         tail = tail[0:6].reshape(3, 2, 1, 2, 1, 128)
-        return (acc.reshape(3, 2, 8, 2, 8, 128) + tail).reshape(3, 16, 16, 128)
+        return (jnp.stack(acc).reshape(3, 2, 8, 2, 8, 128) + tail).reshape(3, 16, 16, 128)
 
     return jax.shard_map(
         per_device,

time: 45.1 us -> 41.5 us (0.920)
  Pallas kernels: 42.5 us -> 39.8 us
  local copies, waits for them, and re-layouts: 1.62 us -> 0.72 us
    pallas_call x1, Pallas kernels: 42.5 us -> 39.8 us  [per_device(): pl.pallas_call(functools.partial(kernel, nw, nn), out_shape=(*[jax.ShapeD...]
    unnamed x4 -> x2, local copies, waits for them, and re-layouts: 1.58 us -> 0.68 us
where the time goes in v2:
time: 41.5 us; the launch traced here: 41.3 us
  Pallas kernels  39.8 us (96%)
  other arithmetic  0.8 us (2%)
  local copies, waits for them, and re-layouts  0.72 us (2%)
    pallas_call x1, Pallas kernels, per_device(): pl.pallas_call(functools.partial(kernel, nw, nn), out_shape=(*[jax.ShapeD...  39.8 us

profile of v2, /device:TPU:1, one launch (start us, length us, event | category | flops | bytes accessed | tf_op | source)
XLA Modules:
  0.0 41.3 jit_solution(7794970125084595446)
XLA Ops:
  0.0 0.0 copy-start
  0.0 0.7 %copy-done = f32[3,3]{1,0:T(4,128)S(1)} copy-done((f32[3,3]{1,0:T(4,128)S(1)}, f32[3,3]{1,0:T(4,128)}, u32[]{:S(2)}) %copy-start) | copy-done | bytes 60
  0.7 39.8 %shard_map.37 = (f32[16,16,128]{2,1,0:T(8,128)S(1)}, f32[16,16,128]{2,1,0:T(8,128)S(1)}, f32[16,16,128]{2,1,0:T(8,128)S(1)}, f32[8,256]{1,0:T(8,128)S(1)}) custom-call(f32[3,16,16,128]{3,2,1,0:T(8,128)} %res.1, f32[16,16,128]{2,1,0:T(8,128)} %stiff.1, f32[3,3]{1,0:T(4,128)S(1)} %copy-done), custom_call_target="tpu_custom_call" | custom-call | tf_op jit(solution)/shard_map/pallas_call | solution.py:646
  40.5 0.8 %maximum_add_fusion = f32[3,16,16,128]{3,2,1,0:T(8,128)} fusion(f32[3,16,16,128]{3,2,1,0:T(8,128)S(1)} %bitcast.9, f32[1,16,16,128]{3,2,1,0:T(8,128)S(1)} %bitcast.7, f32[1,16,16,128]{3,2,1,0:T(8,128)S(1)} %bitcast.6, f32[1,16,16,128]{3,2,1,0:T(8,128)S(1)} %bitcast.5), kind=kLoop, calls=%fused_computation | loop fusion | flops 294912 | bytes 1179648 | tf_op jit(solution)/shard_map/add | solution.py:662
  (2 shorter events, 0.0 us)
Async XLA Ops:
  0.0 0.7 %copy-start = (f32[3,3]{1,0:T(4,128)S(1)}, f32[3,3]{1,0:T(4,128)}, u32[]{:S(2)}) copy-start(f32[3,3]{1,0:T(4,128)} %coup_hbm.1) | copy-start | bytes 112

commit v3 on v2

--- a/solution.py
+++ b/solution.py
@@ -85,13 +85,42 @@
     return out
 
 
+def flat_box_wide(chunks, nz):
+    rows = chunks[0].shape[0]
+    lane = iota(chunks[0].shape, 1)
+    zpos = lane & (nz - 1)
+
+    def shifted(v, y):
+        mid = pltpu.roll(v, y % 128, 1) if y else v
+        return (
+            mid
+            + jnp.where(zpos == 0, 0.0, pltpu.roll(v, (y + 1) % 128, 1))
+            + jnp.where(zpos == nz - 1, 0.0, pltpu.roll(v, (y - 1) % 128, 1))
+        )
+
+    xs = [v + pltpu.roll(v, 1, 0) + pltpu.roll(v, rows - 1, 0) for v in chunks]
+    up = [shifted(v, nz) for v in xs]
+    down = [shifted(v, -nz) for v in xs]
+    out = []
+    for j, v in enumerate(xs):
+        before = up[j - 1] if j > 0 else 0.0
+        after = down[j + 1] if j + 1 < len(xs) else 0.0
+        out.append(
+            shifted(v, 0)
+            + jnp.where(lane < nz, before, up[j])
+            + jnp.where(lane >= 128 - nz, after, down[j])
+        )
+    return out
+
+
 def flat_smooth(f, kappa, coup, level, nz, want_rest):
     theta, steps = chebyshev(level)
     scale = 4.0**-level / 26.0
     n = len(kappa)
 
     def apply(r, d):
-        boxes = [flat_box(d[c], nz) for c in range(3)]
+        box = flat_box if n > 1 else flat_box_wide
+        boxes = [box(d[c], nz) for c in range(3)]
         new = [[None] * n for _ in range(3)]
         for j in range(n):
             u = [27.0 * d[c][j] - boxes[c][j] for c in range(3)]
@@ -132,9 +161,7 @@
     g1b,
     r1,
     e1,
-    w1,
     e2,
-    w2,
     t1,
     u_lo,
     u_hi,
@@ -290,8 +317,11 @@
     def copies1(i, ow, on):
         sx, dx = {0: ((2, 6), (2, 6)), 1: ((4, 6), (0, 2)), -1: ((2, 4), (6, 8))}[ow]
         sy, dy = {0: ((0, 8), (0, 8)), 1: ((4, 8), (12, 16)), -1: ((0, 4), (8, 12))}[on]
-        src = g1.at[:, slice(*sx), slice(*sy), :]
-        return [(src, g1b, (slice(None), slice(*dx), slice(*dy)), s1, q1, i)]
+        sx, dx, sy, dy = slice(*sx), slice(*dx), slice(*sy), slice(*dy)
+        return [
+            (g1.at[0:3, sx, sy], g1b, (slice(0, 3), dx, dy), s1, q1, i),
+            (g1.at[3, sx, sy], g1b, (3, dx, dy), s1, q1, 8 + i),
+        ]
 
     def copies2(i, ow, on):
         dx = slice(4 - 4 * ow, 8 - 4 * ow)
@@ -303,7 +333,8 @@
         return [(h3.at[10:12, :], h3b, (rows,), s3, q3, i)]
 
     def copies4(i, ow, on):
-        return [(h3, h3sb, (5 - on,), s4, q4, i)]
+        rows = slice(0, 22)
+        return [(h3.at[rows], h3sb, (5 - on, rows), s4, q4, i)]
 
     def start(copies, offsets, chosen=None, part=slice(None)):
         for i, (ow, on) in enumerate(offsets):
@@ -382,6 +413,16 @@
         t0[pl.ds(384 + 16 * i, 16), :] = (
             k0[4 + 2 * i, 0:16, :] + k0[5 + 2 * i, 0:16, :]
         )
+
+    def halved(first, count):
+        s = t0[pl.ds(first, count, stride=2), :] + t0[pl.ds(first + 1, count, stride=2), :]
+        s = s.reshape(count // 16, 2, 8, 128)
+        pair = [s[:, u].reshape(count // 2, 128) for u in range(2)]
+        return mm(jnp.concatenate(pair, axis=1), m01[...])
+
+    g1[3, 2:6, 0:8, :] = halved(384, 64).reshape(4, 8, 128)
+    for p in range(4):
+        t1[pl.ds(96 + 8 * p, 8), :] = g1[3, 2 + p, 0:8, :]
 
     theta0, steps0 = chebyshev(0)
     lane24 = iota((24, 128), 1)
@@ -429,15 +470,11 @@
     for k in range(4):
         sweep0(k, (5 + k,), 14 - 2 * k)
     arrive(copies0, NEIGHBOURS, (0, 1, 2, 3, 4, 5))
+    start(copies1, NEIGHBOURS, None, slice(1, 2))
     for k in range(4):
         sweep0(k, (1 + k, 19 - k), 4)
-    s = t0[pl.ds(0, 256, stride=2), :] + t0[pl.ds(1, 256, stride=2), :]
-    s = s.reshape(4, 4, 2, 8, 128)
-    pair = jnp.concatenate(
-        [s[:, :, 0].reshape(128, 128), s[:, :, 1].reshape(128, 128)], axis=1
-    )
-    g1[:, 2:6, 0:8, :] = mm(pair, m01[...]).reshape(4, 4, 8, 128)
-    start(copies1, NEIGHBOURS)
+    g1[0:3, 2:6, 0:8, :] = halved(0, 192).reshape(3, 4, 8, 128)
+    start(copies1, NEIGHBOURS, None, slice(0, 1))
     sent(copies0, NEIGHBOURS)
 
     def sum0(i, carry):
@@ -457,51 +494,40 @@
     theta1, steps1 = chebyshev(1)
     lower = lane16 < 64
     zpos1 = lane16 & 63
-    for p in range(8):
-        for c in range(3):
-            w1[c, p] = pltpu.roll(g1[c, p], 64, 1)
-
-    def plane1(p, d, wd, scale, mass):
+
+    def plane1(p, d, scale, mass):
         us, mids = [], []
         for c in range(3):
             mid = d[c, p]
-            before = wd[c, max(p - 1, 0)]
-            after = wd[c, min(p + 1, 7)]
-            s = mid + wd[c, p] + jnp.where(lower, before, after)
+            swap = mid + jnp.where(lower, d[c, min(p + 1, 7)], d[c, max(p - 1, 0)])
+            up = pltpu.roll(mid, 1, 1) + pltpu.roll(swap, 65, 1)
+            down = pltpu.roll(mid, 127, 1) + pltpu.roll(swap, 63, 1)
+            s = mid + pltpu.roll(swap, 64, 1)
+            s = s + jnp.where(zpos1 == 0, 0.0, up) + jnp.where(zpos1 == 63, 0.0, down)
             s = s + pltpu.roll(s, 1, 0) + pltpu.roll(s, 15, 0)
-            s = (
-                s
-                + jnp.where(zpos1 == 0, 0.0, pltpu.roll(s, 1, 1))
-                + jnp.where(zpos1 == 63, 0.0, pltpu.roll(s, 127, 1))
-            )
             us.append(27.0 * mid - s)
             mids.append(mid)
         return mids, mix(coup, scale, mass, us, mids, g1[3, p])
 
     x1 = {}
-    pairs1 = [(g1, w1), (e1, w2), (e2, w1), (e1, w2)]
+    fields1 = [g1, e1, e2, e1]
     for k, (lo, hi) in enumerate([(0, 8), (1, 7), (1, 7), (2, 6)]):
-        d, wd = pairs1[k]
+        d = fields1[k]
         over = 1.0 / theta1 if k == 0 else 1.0
         scale, mass = over / (4.0 * 26.0), over * MASS
         for p in range(lo, hi):
-            mids, a = plane1(p, d, wd, scale, mass)
+            mids, a = plane1(p, d, scale, mass)
             for c in range(3):
                 new = (g1 if k == 0 else r1)[c, p] - a[c]
                 if k < 3:
                     ca, cb = steps1[k]
-                    nd, nwd = pairs1[k + 1]
                     r1[c, p] = new
-                    step = (ca * over) * mids[c] + cb * new
-                    nd[c, p] = step
-                    nwd[c, p] = pltpu.roll(step, 64, 1)
+                    fields1[k + 1][c, p] = (ca * over) * mids[c] + cb * new
                 else:
                     t1[pl.ds(32 * c + 8 * (p - 2), 8), :] = new[0:8]
                 if 2 <= p < 6:
                     part = (mids[c] * over)[0:8]
                     x1[c, p] = part if k == 0 else x1[c, p] + part
-    for p in range(4):
-        t1[pl.ds(96 + 8 * p, 8), :] = g1[3, 2 + p, 0:8, :]
 
     ys = [t1[pl.ds(y, 16, stride=8), :] for y in range(8)]
     ys = jnp.concatenate([ys[2 * j] + ys[2 * j + 1] for j in range(4)], axis=1)
@@ -568,19 +594,22 @@
             f3[c][v] = out
     x3, r3 = flat_smooth(f3[:3], f3[3], coup, 3, 16, True)
 
+    z4[...] = mm(
+        jnp.concatenate(
+            [jnp.concatenate(r3[c] if c < 3 else f3[3], axis=1) for c in range(4)],
+            axis=0,
+        ),
+        m34[...],
+    )
+    f4 = []
     for c in range(4):
-        src = jnp.concatenate(r3[c] if c < 3 else f3[3], axis=1)
-        t3[24 * c : 24 * c + 24, :] = src
-    s = mm(t3[...], m34[...])
-    z4[...] = s
-    s = z4[pl.ds(0, 48, stride=2), :] + z4[pl.ds(1, 48, stride=2), :]
-    pad = jnp.zeros((4, 128), F32)
-    f4 = [[jnp.concatenate([s[12 * c : 12 * c + 12], pad], axis=0)] for c in range(4)]
+        even, odd = (z4[pl.ds(24 * c + 4 + u, 8, stride=2), :] for u in range(2))
+        f4.append([even + odd])
     x4, _ = flat_smooth(f4[:3], f4[3], coup, 4, 8, False)
 
     for c in range(3):
         t3[2 * c : 2 * c + 2, 0:128] = x3[c][1][10:12]
-        t3[2 * c : 2 * c + 2, 128:256] = jnp.broadcast_to(x4[c][0][5:6], (2, 128))
+        t3[2 * c : 2 * c + 2, 128:256] = jnp.broadcast_to(x4[c][0][3:4], (2, 128))
     tail_out[...] = mm(t3[0:16, 0:256], p34[...])[0:8]
 
 
@@ -606,8 +635,6 @@
         vm(3, 8, 16, 128),
         vm(3, 8, 16, 128),
         vm(3, 8, 16, 128),
-        vm(3, 8, 16, 128),
-        vm(3, 8, 16, 128),
         vm(128, 128),
         vm(192, 128),
         vm(192, 128),
@@ -616,7 +643,7 @@
         vm(256, 128),
         vm(2, 24, 128),
         vm(2, 11, 24, 128),
-        vm(96, 384),
+        vm(16, 256),
         vm(96, 128),
         mat(256, 128),
         mat(512, 128),
@@ -630,8 +657,8 @@
         pltpu.SemaphoreType.REGULAR,
         dma((16,)),
         dma((16,)),
-        dma((8,)),
-        dma((8,)),
+        dma((16,)),
+        dma((16,)),
         dma((8,)),
         dma((8,)),
         dma((10,)),

time: 41.5 us -> 41.4 us (level)
  no operation moved by 1% of the time
where the time goes in v3:
time: 41.4 us; the launch traced here: 41.2 us
  Pallas kernels  39.7 us (96%)
  other arithmetic  0.8 us (2%)
  local copies, waits for them, and re-layouts  0.72 us (2%)
    pallas_call x1, Pallas kernels, per_device(): pl.pallas_call(functools.partial(kernel, nw, nn), out_shape=(*[jax.ShapeD...  39.7 us

profile of v3, /device:TPU:1, one launch (start us, length us, event | category | flops | bytes accessed | tf_op | source)
XLA Modules:
  0.0 41.2 jit_solution(8425581139813553570)
XLA Ops:
  0.0 0.0 copy-start
  0.0 0.7 %copy-done = f32[3,3]{1,0:T(4,128)S(1)} copy-done((f32[3,3]{1,0:T(4,128)S(1)}, f32[3,3]{1,0:T(4,128)}, u32[]{:S(2)}) %copy-start) | copy-done | bytes 60
  0.7 39.7 %shard_map.37 = (f32[16,16,128]{2,1,0:T(8,128)S(1)}, f32[16,16,128]{2,1,0:T(8,128)S(1)}, f32[16,16,128]{2,1,0:T(8,128)S(1)}, f32[8,256]{1,0:T(8,128)S(1)}) custom-call(f32[3,16,16,128]{3,2,1,0:T(8,128)} %res.1, f32[16,16,128]{2,1,0:T(8,128)} %stiff.1, f32[3,3]{1,0:T(4,128)S(1)} %copy-done), custom_call_target="tpu_custom_call" | custom-call | tf_op jit(solution)/shard_map/pallas_call | solution.py:673
  40.4 0.8 %maximum_add_fusion = f32[3,16,16,128]{3,2,1,0:T(8,128)} fusion(f32[3,16,16,128]{3,2,1,0:T(8,128)S(1)} %bitcast.9, f32[1,16,16,128]{3,2,1,0:T(8,128)S(1)} %bitcast.7, f32[1,16,16,128]{3,2,1,0:T(8,128)S(1)} %bitcast.6, f32[1,16,16,128]{3,2,1,0:T(8,128)S(1)} %bitcast.5), kind=kLoop, calls=%fused_computation | loop fusion | flops 294912 | bytes 1179648 | tf_op jit(solution)/shard_map/add | solution.py:689
  (2 shorter events, 0.0 us)
Async XLA Ops:
  0.0 0.7 %copy-start = (f32[3,3]{1,0:T(4,128)S(1)}, f32[3,3]{1,0:T(4,128)}, u32[]{:S(2)}) copy-start(f32[3,3]{1,0:T(4,128)} %coup_hbm.1) | copy-start | bytes 112

commit v4 on v3

--- a/solution.py
+++ b/solution.py
@@ -12,7 +12,7 @@
 RATIO = 8.0
 MESH = pl.DeviceIdType.MESH
 NEIGHBOURS = [(1, 1), (1, -1), (-1, 1), (-1, -1), (1, 0), (-1, 0), (0, 1), (0, -1)]
-AXIAL = NEIGHBOURS[4:]
+NEAR = NEIGHBOURS + [(2, 0), (-2, 0), (0, 2), (0, -2)]
 WINDOW = [o for k in range(5, 0, -1) for o in (k, -k)]
 F32 = jnp.float32
 BF16 = jnp.bfloat16
@@ -181,7 +181,6 @@
     p34,
     coup_ref,
     local_sem,
-    ready_sem,
     s0,
     q0,
     s1,
@@ -289,12 +288,12 @@
             )
 
     barrier = pltpu.get_barrier_semaphore()
-    tell(barrier, AXIAL)
+    tell(barrier, NEAR)
     g1[...] = jnp.zeros_like(g1)
     g2[...] = jnp.zeros_like(g2)
     own_f.wait()
     own_k.wait()
-    pl.semaphore_wait(barrier, len(AXIAL))
+    pl.semaphore_wait(barrier, len(NEAR))
 
     def copies0(i, ow, on):
         sx, dx = {0: (0, 4), 1: (12, 0), -1: (0, 20)}[ow]
@@ -358,12 +357,9 @@
     along_wide = [(o, 0) for o in WINDOW]
     along_narrow = [(0, o) for o in WINDOW]
 
-    start(copies0, NEIGHBOURS, (4, 5), slice(0, 1))
     start(copies0, NEIGHBOURS, (6, 7))
-    tell(ready_sem, AXIAL)
-    pl.semaphore_wait(ready_sem, len(AXIAL))
     start(copies0, NEIGHBOURS, (0, 1, 2, 3))
-    start(copies0, NEIGHBOURS, (4, 5), slice(1, 2))
+    start(copies0, NEIGHBOURS, (4, 5))
 
     @pl.when(w == 0)
     def _():
@@ -654,7 +650,6 @@
         mat(256, 256),
         pltpu.SMEM((3, 3), F32),
         dma((3,)),
-        pltpu.SemaphoreType.REGULAR,
         dma((16,)),
         dma((16,)),
         dma((16,)),

time: 41.4 us -> 42.3 us (1.022)
  Pallas kernels: 39.7 us -> 40.4 us
    pallas_call x1, Pallas kernels: 39.7 us -> 40.4 us  [per_device(): pl.pallas_call(functools.partial(kernel, nw, nn), out_shape=(*[jax.ShapeD...]
where the time goes in v4:
time: 42.3 us; the launch traced here: 41.9 us
  Pallas kernels  40.4 us (96%)
  other arithmetic  0.8 us (2%)
  local copies, waits for them, and re-layouts  0.72 us (2%)
    pallas_call x1, Pallas kernels, per_device(): pl.pallas_call(functools.partial(kernel, nw, nn), out_shape=(*[jax.ShapeD...  40.4 us

profile of v4, /device:TPU:1, one launch (start us, length us, event | category | flops | bytes accessed | tf_op | source)
XLA Modules:
  0.0 41.9 jit_solution(14036729252685123160)
XLA Ops:
  0.0 0.0 copy-start
  0.0 0.7 %copy-done = f32[3,3]{1,0:T(4,128)S(1)} copy-done((f32[3,3]{1,0:T(4,128)S(1)}, f32[3,3]{1,0:T(4,128)}, u32[]{:S(2)}) %copy-start) | copy-done | bytes 60
  0.7 40.4 %shard_map.37 = (f32[16,16,128]{2,1,0:T(8,128)S(1)}, f32[16,16,128]{2,1,0:T(8,128)S(1)}, f32[16,16,128]{2,1,0:T(8,128)S(1)}, f32[8,256]{1,0:T(8,128)S(1)}) custom-call(f32[3,16,16,128]{3,2,1,0:T(8,128)} %res.1, f32[16,16,128]{2,1,0:T(8,128)} %stiff.1, f32[3,3]{1,0:T(4,128)S(1)} %copy-done), custom_call_target="tpu_custom_call" | custom-call | tf_op jit(solution)/shard_map/pallas_call | solution.py:668
  41.1 0.8 %maximum_add_fusion = f32[3,16,16,128]{3,2,1,0:T(8,128)} fusion(f32[3,16,16,128]{3,2,1,0:T(8,128)S(1)} %bitcast.9, f32[1,16,16,128]{3,2,1,0:T(8,128)S(1)} %bitcast.7, f32[1,16,16,128]{3,2,1,0:T(8,128)S(1)} %bitcast.6, f32[1,16,16,128]{3,2,1,0:T(8,128)S(1)} %bitcast.5), kind=kLoop, calls=%fused_computation | loop fusion | flops 294912 | bytes 1179648 | tf_op jit(solution)/shard_map/add | solution.py:684
  (2 shorter events, 0.0 us)
Async XLA Ops:
  0.0 0.7 %copy-start = (f32[3,3]{1,0:T(4,128)S(1)}, f32[3,3]{1,0:T(4,128)}, u32[]{:S(2)}) copy-start(f32[3,3]{1,0:T(4,128)} %coup_hbm.1) | copy-start | bytes 112

commit v5 on v3

--- a/solution.py
+++ b/solution.py
@@ -292,26 +292,24 @@
     tell(barrier, AXIAL)
     g1[...] = jnp.zeros_like(g1)
     g2[...] = jnp.zeros_like(g2)
-    own_f.wait()
-    own_k.wait()
     pl.semaphore_wait(barrier, len(AXIAL))
 
     def copies0(i, ow, on):
         sx, dx = {0: (0, 4), 1: (12, 0), -1: (0, 20)}[ow]
         sy, dy = {0: (0, 0), 1: (12, 20), -1: (0, 16)}[on]
         nx, ny = (16 if ow == 0 else 4), (16 if on == 0 else 4)
-        fs = (slice(None), slice(4 + sx, 4 + sx + nx), slice(sy, sy + ny))
+        fs = (slice(None), slice(sx, sx + nx), slice(sy, sy + ny))
         fd = (slice(None), slice(dx, dx + nx), slice(dy, dy + ny))
         if ow > 0:
             sx, dx = sx + 1, dx + 1
         if on > 0:
             sy, dy = sy + 1, dy + 1
         nx, ny = (16 if ow == 0 else 3), (16 if on == 0 else 3)
-        ks = (slice(4 + sx, 4 + sx + nx), slice(sy, sy + ny))
+        ks = (slice(sx, sx + nx), slice(sy, sy + ny))
         kd = (slice(dx, dx + nx), slice(dy, dy + ny))
         return [
-            (f0.at[fs], f0b, fd, s0, q0, i),
-            (k0.at[ks], k0b, kd, s0, q0, 8 + i),
+            (res.at[fs], f0b, fd, s0, q0, i),
+            (stiff.at[ks], k0b, kd, s0, q0, 8 + i),
         ]
 
     def copies1(i, ow, on):
@@ -409,6 +407,7 @@
     own_c.wait()
     coup = [[coup_ref[i, j] for j in range(3)] for i in range(3)]
 
+    own_k.wait()
     for i in range(8):
         t0[pl.ds(384 + 16 * i, 16), :] = (
             k0[4 + 2 * i, 0:16, :] + k0[5 + 2 * i, 0:16, :]
@@ -466,6 +465,7 @@
                     for c in range(3):
                         t0[pl.ds(128 * c + 8 * (i - 4), 16), :] = new[0][c] + new[1][c]
 
+    own_f.wait()
     arrive(copies0, NEIGHBOURS, (6, 7))
     for k in range(4):
         sweep0(k, (5 + k,), 14 - 2 * k)

time: 41.4 us -> 41.5 us (level)
  no operation moved by 1% of the time
where the time goes in v5:
time: 41.5 us; the launch traced here: 41.4 us
  Pallas kernels  39.9 us (96%)
  other arithmetic  0.8 us (2%)
  local copies, waits for them, and re-layouts  0.72 us (2%)
    pallas_call x1, Pallas kernels, per_device(): pl.pallas_call(functools.partial(kernel, nw, nn), out_shape=(*[jax.ShapeD...  39.9 us

profile of v5, /device:TPU:1, one launch (start us, length us, event | category | flops | bytes accessed | tf_op | source)
XLA Modules:
  0.0 41.4 jit_solution(13192372171864161684)
XLA Ops:
  0.0 0.0 copy-start
  0.0 0.7 %copy-done = f32[3,3]{1,0:T(4,128)S(1)} copy-done((f32[3,3]{1,0:T(4,128)S(1)}, f32[3,3]{1,0:T(4,128)}, u32[]{:S(2)}) %copy-start) | copy-done | bytes 60
  0.7 39.9 %shard_map.37 = (f32[16,16,128]{2,1,0:T(8,128)S(1)}, f32[16,16,128]{2,1,0:T(8,128)S(1)}, f32[16,16,128]{2,1,0:T(8,128)S(1)}, f32[8,256]{1,0:T(8,128)S(1)}) custom-call(f32[3,16,16,128]{3,2,1,0:T(8,128)} %res.1, f32[16,16,128]{2,1,0:T(8,128)} %stiff.1, f32[3,3]{1,0:T(4,128)S(1)} %copy-done), custom_call_target="tpu_custom_call" | custom-call | tf_op jit(solution)/shard_map/pallas_call | solution.py:673
  40.6 0.8 %maximum_add_fusion = f32[3,16,16,128]{3,2,1,0:T(8,128)} fusion(f32[3,16,16,128]{3,2,1,0:T(8,128)S(1)} %bitcast.9, f32[1,16,16,128]{3,2,1,0:T(8,128)S(1)} %bitcast.7, f32[1,16,16,128]{3,2,1,0:T(8,128)S(1)} %bitcast.6, f32[1,16,16,128]{3,2,1,0:T(8,128)S(1)} %bitcast.5), kind=kLoop, calls=%fused_computation | loop fusion | flops 294912 | bytes 1179648 | tf_op jit(solution)/shard_map/add | solution.py:689
  (2 shorter events, 0.0 us)
Async XLA Ops:
  0.0 0.7 %copy-start = (f32[3,3]{1,0:T(4,128)S(1)}, f32[3,3]{1,0:T(4,128)}, u32[]{:S(2)}) copy-start(f32[3,3]{1,0:T(4,128)} %coup_hbm.1) | copy-start | bytes 112

commit v6 on v3

--- a/solution.py
+++ b/solution.py
@@ -268,12 +268,14 @@
             device_id_type=MESH,
         )
 
-    own_f = pltpu.make_async_copy(res, f0.at[:, 4:20, 0:16, :], local_sem.at[0])
+    own_f = [
+        pltpu.make_async_copy(res.at[c], f0.at[c, 4:20, 0:16, :], local_sem.at[2 + c])
+        for c in range(3)
+    ]
     own_k = pltpu.make_async_copy(stiff, k0.at[4:20, 0:16, :], local_sem.at[1])
-    own_c = pltpu.make_async_copy(coup_hbm, coup_ref, local_sem.at[2])
-    own_f.start()
-    own_k.start()
-    own_c.start()
+    own_c = pltpu.make_async_copy(coup_hbm, coup_ref, local_sem.at[0])
+    for c in own_f:
+        c.start()
 
     h3[...] = jnp.zeros_like(h3)
     h3s[...] = jnp.zeros_like(h3s)
@@ -290,9 +292,12 @@
 
     barrier = pltpu.get_barrier_semaphore()
     tell(barrier, AXIAL)
+    own_k.start()
+    own_c.start()
     g1[...] = jnp.zeros_like(g1)
     g2[...] = jnp.zeros_like(g2)
-    own_f.wait()
+    for c in own_f:
+        c.wait()
     own_k.wait()
     pl.semaphore_wait(barrier, len(AXIAL))
 
@@ -359,11 +364,12 @@
     along_narrow = [(0, o) for o in WINDOW]
 
     start(copies0, NEIGHBOURS, (4, 5), slice(0, 1))
+    tell(ready_sem.at[0], AXIAL)
     start(copies0, NEIGHBOURS, (6, 7))
-    tell(ready_sem, AXIAL)
-    pl.semaphore_wait(ready_sem, len(AXIAL))
+    start(copies0, NEIGHBOURS, (4, 5), slice(1, 2))
+    pl.semaphore_wait(ready_sem.at[0], len(AXIAL))
     start(copies0, NEIGHBOURS, (0, 1, 2, 3))
-    start(copies0, NEIGHBOURS, (4, 5), slice(1, 2))
+    tell(ready_sem.at[1], AXIAL)
 
     @pl.when(w == 0)
     def _():
@@ -470,6 +476,7 @@
     for k in range(4):
         sweep0(k, (5 + k,), 14 - 2 * k)
     arrive(copies0, NEIGHBOURS, (0, 1, 2, 3, 4, 5))
+    pl.semaphore_wait(ready_sem.at[1], len(AXIAL))
     start(copies1, NEIGHBOURS, None, slice(1, 2))
     for k in range(4):
         sweep0(k, (1 + k, 19 - k), 4)
@@ -610,7 +617,9 @@
     for c in range(3):
         t3[2 * c : 2 * c + 2, 0:128] = x3[c][1][10:12]
         t3[2 * c : 2 * c + 2, 128:256] = jnp.broadcast_to(x4[c][0][3:4], (2, 128))
-    tail_out[...] = mm(t3[0:16, 0:256], p34[...])[0:8]
+    tail_out[...] = (
+        mm(t3[0:16, 0:128], p34[0:128, :]) + mm(t3[0:16, 128:256], p34[128:256, :])
+    )[0:8]
 
 
 def solution(mesh):
@@ -653,8 +662,8 @@
         mat(128, 512),
         mat(256, 256),
         pltpu.SMEM((3, 3), F32),
-        dma((3,)),
-        pltpu.SemaphoreType.REGULAR,
+        dma((5,)),
+        pltpu.SemaphoreType.REGULAR((2,)),
         dma((16,)),
         dma((16,)),
         dma((16,)),

time: 41.4 us -> 41.4 us (level)
  no operation moved by 1% of the time
where the time goes in v6:
time: 41.4 us; the launch traced here: 41.2 us
  Pallas kernels  39.7 us (96%)
  other arithmetic  0.8 us (2%)
  local copies, waits for them, and re-layouts  0.72 us (2%)
    pallas_call x1, Pallas kernels, per_device(): pl.pallas_call(functools.partial(kernel, nw, nn), out_shape=(*[jax.ShapeD...  39.7 us

profile of v6, /device:TPU:1, one launch (start us, length us, event | category | flops | bytes accessed | tf_op | source)
XLA Modules:
  0.0 41.2 jit_solution(816938768192654067)
XLA Ops:
  0.0 0.0 copy-start
  0.0 0.7 %copy-done = f32[3,3]{1,0:T(4,128)S(1)} copy-done((f32[3,3]{1,0:T(4,128)S(1)}, f32[3,3]{1,0:T(4,128)}, u32[]{:S(2)}) %copy-start) | copy-done | bytes 60
  0.7 39.7 %shard_map.37 = (f32[16,16,128]{2,1,0:T(8,128)S(1)}, f32[16,16,128]{2,1,0:T(8,128)S(1)}, f32[16,16,128]{2,1,0:T(8,128)S(1)}, f32[8,256]{1,0:T(8,128)S(1)}) custom-call(f32[3,16,16,128]{3,2,1,0:T(8,128)} %res.1, f32[16,16,128]{2,1,0:T(8,128)} %stiff.1, f32[3,3]{1,0:T(4,128)S(1)} %copy-done), custom_call_target="tpu_custom_call" | custom-call | tf_op jit(solution)/shard_map/pallas_call | solution.py:682
  40.4 0.8 %maximum_add_fusion = f32[3,16,16,128]{3,2,1,0:T(8,128)} fusion(f32[3,16,16,128]{3,2,1,0:T(8,128)S(1)} %bitcast.9, f32[1,16,16,128]{3,2,1,0:T(8,128)S(1)} %bitcast.7, f32[1,16,16,128]{3,2,1,0:T(8,128)S(1)} %bitcast.6, f32[1,16,16,128]{3,2,1,0:T(8,128)S(1)} %bitcast.5), kind=kLoop, calls=%fused_computation | loop fusion | flops 294912 | bytes 1179648 | tf_op jit(solution)/shard_map/add | solution.py:698
  (2 shorter events, 0.0 us)
Async XLA Ops:
  0.0 0.7 %copy-start = (f32[3,3]{1,0:T(4,128)S(1)}, f32[3,3]{1,0:T(4,128)}, u32[]{:S(2)}) copy-start(f32[3,3]{1,0:T(4,128)} %coup_hbm.1) | copy-start | bytes 112

commit v7 on v6

--- a/solution.py
+++ b/solution.py
@@ -334,12 +334,15 @@
         return [(g2.at[:, 4:8, 128:256], g2b, (slice(None), dx, dy), s2, q2, i)]
 
     def copies3(i, ow, on):
-        rows = slice(10 - 2 * ow, 12 - 2 * ow)
-        return [(h3.at[10:12, :], h3b, (rows,), s3, q3, i)]
+        row = (6 - 2 * ow) % 24
+        return [(h3.at[6:8, :], h3b, (slice(row, row + 2),), s3, q3, i)]
 
     def copies4(i, ow, on):
-        rows = slice(0, 22)
-        return [(h3.at[rows], h3sb, (5 - on, rows), s4, q4, i)]
+        near, far = slice(0, 12), slice(12, 24)
+        return [
+            (h3.at[near], h3sb, (5 - on, near), s4, q4, i),
+            (h3.at[far], h3sb, (5 - on, far), s4, q4, 10 + i),
+        ]
 
     def start(copies, offsets, chosen=None, part=slice(None)):
         for i, (ow, on) in enumerate(offsets):
@@ -564,7 +567,7 @@
     t2[...] = mm(
         jnp.concatenate([r2[0][1], r2[1][1], r2[2][1], f2[3][1]], axis=1), m23[...]
     )
-    h3[10:12, :] = t2[pl.ds(4, 2, stride=2), :] + t2[pl.ds(5, 2, stride=2), :]
+    h3[6:8, :] = t2[pl.ds(4, 2, stride=2), :] + t2[pl.ds(5, 2, stride=2), :]
     start(copies3, along_wide)
     sent(copies2, NEIGHBOURS)
 
@@ -580,8 +583,12 @@
             for j in range(4):
                 acc[c][4 * k + j] += part
 
-    arrive(copies3, along_wide)
-    start(copies4, along_narrow)
+    close = [i for i, (ow, _) in enumerate(along_wide) if -2 <= ow <= 3]
+    apart = [i for i in range(len(along_wide)) if i not in close]
+    arrive(copies3, along_wide, close)
+    start(copies4, along_narrow, None, slice(0, 1))
+    arrive(copies3, along_wide, apart)
+    start(copies4, along_narrow, None, slice(1, 2))
     sent(copies3, along_wide)
     arrive(copies4, along_narrow)
     sent(copies4, along_narrow)
@@ -610,12 +617,12 @@
     )
     f4 = []
     for c in range(4):
-        even, odd = (z4[pl.ds(24 * c + 4 + u, 8, stride=2), :] for u in range(2))
+        even, odd = (z4[pl.ds(24 * c + u, 8, stride=2), :] for u in range(2))
         f4.append([even + odd])
     x4, _ = flat_smooth(f4[:3], f4[3], coup, 4, 8, False)
 
     for c in range(3):
-        t3[2 * c : 2 * c + 2, 0:128] = x3[c][1][10:12]
+        t3[2 * c : 2 * c + 2, 0:128] = x3[c][1][6:8]
         t3[2 * c : 2 * c + 2, 128:256] = jnp.broadcast_to(x4[c][0][3:4], (2, 128))
     tail_out[...] = (
         mm(t3[0:16, 0:128], p34[0:128, :]) + mm(t3[0:16, 128:256], p34[128:256, :])
@@ -672,8 +679,8 @@
         dma((8,)),
         dma((10,)),
         dma((10,)),
-        dma((10,)),
-        dma((10,)),
+        dma((20,)),
+        dma((20,)),
     ]
 
     def per_device(residual, stiffness, coupling):

time: 41.4 us -> 41.5 us (level)
  no operation moved by 1% of the time
where the time goes in v7:
time: 41.5 us; the launch traced here: 41.3 us
  Pallas kernels  39.8 us (96%)
  other arithmetic  0.8 us (2%)
  local copies, waits for them, and re-layouts  0.72 us (2%)
    pallas_call x1, Pallas kernels, per_device(): pl.pallas_call(functools.partial(kernel, nw, nn), out_shape=(*[jax.ShapeD...  39.8 us

profile of v7, /device:TPU:1, one launch (start us, length us, event | category | flops | bytes accessed | tf_op | source)
XLA Modules:
  0.0 41.3 jit_solution(12853095928067449797)
XLA Ops:
  0.0 0.0 copy-start
  0.0 0.7 %copy-done = f32[3,3]{1,0:T(4,128)S(1)} copy-done((f32[3,3]{1,0:T(4,128)S(1)}, f32[3,3]{1,0:T(4,128)}, u32[]{:S(2)}) %copy-start) | copy-done | bytes 60
  0.7 39.8 %shard_map.37 = (f32[16,16,128]{2,1,0:T(8,128)S(1)}, f32[16,16,128]{2,1,0:T(8,128)S(1)}, f32[16,16,128]{2,1,0:T(8,128)S(1)}, f32[8,256]{1,0:T(8,128)S(1)}) custom-call(f32[3,16,16,128]{3,2,1,0:T(8,128)} %res.1, f32[16,16,128]{2,1,0:T(8,128)} %stiff.1, f32[3,3]{1,0:T(4,128)S(1)} %copy-done), custom_call_target="tpu_custom_call" | custom-call | tf_op jit(solution)/shard_map/pallas_call | solution.py:689
  40.5 0.8 %maximum_add_fusion = f32[3,16,16,128]{3,2,1,0:T(8,128)} fusion(f32[3,16,16,128]{3,2,1,0:T(8,128)S(1)} %bitcast.9, f32[1,16,16,128]{3,2,1,0:T(8,128)S(1)} %bitcast.7, f32[1,16,16,128]{3,2,1,0:T(8,128)S(1)} %bitcast.6, f32[1,16,16,128]{3,2,1,0:T(8,128)S(1)} %bitcast.5), kind=kLoop, calls=%fused_computation | loop fusion | flops 294912 | bytes 1179648 | tf_op jit(solution)/shard_map/add | solution.py:705
  (2 shorter events, 0.0 us)
Async XLA Ops:
  0.0 0.7 %copy-start = (f32[3,3]{1,0:T(4,128)S(1)}, f32[3,3]{1,0:T(4,128)}, u32[]{:S(2)}) copy-start(f32[3,3]{1,0:T(4,128)} %coup_hbm.1) | copy-start | bytes 112

commit v8 on v3

--- a/solution.py
+++ b/solution.py
@@ -275,6 +275,7 @@
     own_k.start()
     own_c.start()
 
+    g1[...] = jnp.zeros_like(g1)
     h3[...] = jnp.zeros_like(h3)
     h3s[...] = jnp.zeros_like(h3s)
 
@@ -290,7 +291,6 @@
 
     barrier = pltpu.get_barrier_semaphore()
     tell(barrier, AXIAL)
-    g1[...] = jnp.zeros_like(g1)
     g2[...] = jnp.zeros_like(g2)
     own_f.wait()
     own_k.wait()
@@ -357,6 +357,8 @@
 
     along_wide = [(o, 0) for o in WINDOW]
     along_narrow = [(0, o) for o in WINDOW]
+    for ow, on in along_wide + along_narrow:
+        target(ow, on)
 
     start(copies0, NEIGHBOURS, (4, 5), slice(0, 1))
     start(copies0, NEIGHBOURS, (6, 7))
@@ -469,8 +471,8 @@
     arrive(copies0, NEIGHBOURS, (6, 7))
     for k in range(4):
         sweep0(k, (5 + k,), 14 - 2 * k)
+    start(copies1, NEIGHBOURS, None, slice(1, 2))
     arrive(copies0, NEIGHBOURS, (0, 1, 2, 3, 4, 5))
-    start(copies1, NEIGHBOURS, None, slice(1, 2))
     for k in range(4):
         sweep0(k, (1 + k, 19 - k), 4)
     g1[0:3, 2:6, 0:8, :] = halved(0, 192).reshape(3, 4, 8, 128)

time: 41.4 us -> 41.3 us (level)
  no operation moved by 1% of the time
where the time goes in v8:
time: 41.3 us; the launch traced here: 41.2 us
  Pallas kernels  39.6 us (96%)
  other arithmetic  0.8 us (2%)
  local copies, waits for them, and re-layouts  0.72 us (2%)
    pallas_call x1, Pallas kernels, per_device(): pl.pallas_call(functools.partial(kernel, nw, nn), out_shape=(*[jax.ShapeD...  39.6 us

profile of v8, /device:TPU:1, one launch (start us, length us, event | category | flops | bytes accessed | tf_op | source)
XLA Modules:
  0.0 41.2 jit_solution(13984230956936087701)
XLA Ops:
  0.0 0.0 copy-start
  0.0 0.7 %copy-done = f32[3,3]{1,0:T(4,128)S(1)} copy-done((f32[3,3]{1,0:T(4,128)S(1)}, f32[3,3]{1,0:T(4,128)}, u32[]{:S(2)}) %copy-start) | copy-done | bytes 60
  0.7 39.6 %shard_map.37 = (f32[16,16,128]{2,1,0:T(8,128)S(1)}, f32[16,16,128]{2,1,0:T(8,128)S(1)}, f32[16,16,128]{2,1,0:T(8,128)S(1)}, f32[8,256]{1,0:T(8,128)S(1)}) custom-call(f32[3,16,16,128]{3,2,1,0:T(8,128)} %res.1, f32[16,16,128]{2,1,0:T(8,128)} %stiff.1, f32[3,3]{1,0:T(4,128)S(1)} %copy-done), custom_call_target="tpu_custom_call" | custom-call | tf_op jit(solution)/shard_map/pallas_call | solution.py:675
  40.4 0.8 %maximum_add_fusion = f32[3,16,16,128]{3,2,1,0:T(8,128)} fusion(f32[3,16,16,128]{3,2,1,0:T(8,128)S(1)} %bitcast.9, f32[1,16,16,128]{3,2,1,0:T(8,128)S(1)} %bitcast.7, f32[1,16,16,128]{3,2,1,0:T(8,128)S(1)} %bitcast.6, f32[1,16,16,128]{3,2,1,0:T(8,128)S(1)} %bitcast.5), kind=kLoop, calls=%fused_computation | loop fusion | flops 294912 | bytes 1179648 | tf_op jit(solution)/shard_map/add | solution.py:691
  (2 shorter events, 0.0 us)
Async XLA Ops:
  0.0 0.7 %copy-start = (f32[3,3]{1,0:T(4,128)S(1)}, f32[3,3]{1,0:T(4,128)}, u32[]{:S(2)}) copy-start(f32[3,3]{1,0:T(4,128)} %coup_hbm.1) | copy-start | bytes 112

commit v9 on v3

--- a/solution.py
+++ b/solution.py
@@ -554,7 +554,7 @@
     f2 = [[g2[c, :, 128 * j : 128 * j + 128] for j in range(3)] for c in range(4)]
     x2, r2 = flat_smooth(f2[:3], f2[3], coup, 2, 32, True)
 
-    t2[...] = mm(
+    t2[0:16, :] = mm(
         jnp.concatenate([r2[0][1], r2[1][1], r2[2][1], f2[3][1]], axis=1), m23[...]
     )
     h3[10:12, :] = t2[pl.ds(4, 2, stride=2), :] + t2[pl.ds(5, 2, stride=2), :]
@@ -594,7 +594,7 @@
             f3[c][v] = out
     x3, r3 = flat_smooth(f3[:3], f3[3], coup, 3, 16, True)
 
-    z4[...] = mm(
+    z4[0:96, :] = mm(
         jnp.concatenate(
             [jnp.concatenate(r3[c] if c < 3 else f3[3], axis=1) for c in range(4)],
             axis=0,
@@ -630,21 +630,21 @@
         vm(3, 24, 24, 128),
         vm(3, 24, 24, 128),
         vm(3, 24, 24, 128),
-        vm(512, 128),
+        vm(528, 128),
         vm(2, 4, 8, 16, 128),
         vm(3, 8, 16, 128),
         vm(3, 8, 16, 128),
         vm(3, 8, 16, 128),
-        vm(128, 128),
-        vm(192, 128),
-        vm(192, 128),
+        vm(144, 128),
+        vm(208, 128),
+        vm(208, 128),
         vm(2, 4, 16, 384),
-        vm(16, 128),
-        vm(256, 128),
+        vm(32, 128),
+        vm(288, 128),
         vm(2, 24, 128),
         vm(2, 11, 24, 128),
         vm(16, 256),
-        vm(96, 128),
+        vm(128, 128),
         mat(256, 128),
         mat(512, 128),
         mat(512, 128),

time: 41.4 us -> 41.3 us (level)
  no operation moved by 1% of the time
where the time goes in v9:
time: 41.3 us; the launch traced here: 41.2 us
  Pallas kernels  39.7 us (96%)
  other arithmetic  0.8 us (2%)
  local copies, waits for them, and re-layouts  0.72 us (2%)
    pallas_call x1, Pallas kernels, per_device(): pl.pallas_call(functools.partial(kernel, nw, nn), out_shape=(*[jax.ShapeD...  39.7 us

profile of v9, /device:TPU:1, one launch (start us, length us, event | category | flops | bytes accessed | tf_op | source)
XLA Modules:
  0.0 41.2 jit_solution(12807858413748515878)
XLA Ops:
  0.0 0.0 copy-start
  0.0 0.7 %copy-done = f32[3,3]{1,0:T(4,128)S(1)} copy-done((f32[3,3]{1,0:T(4,128)S(1)}, f32[3,3]{1,0:T(4,128)}, u32[]{:S(2)}) %copy-start) | copy-done | bytes 60
  0.7 39.7 %shard_map.37 = (f32[16,16,128]{2,1,0:T(8,128)S(1)}, f32[16,16,128]{2,1,0:T(8,128)S(1)}, f32[16,16,128]{2,1,0:T(8,128)S(1)}, f32[8,256]{1,0:T(8,128)S(1)}) custom-call(f32[3,16,16,128]{3,2,1,0:T(8,128)} %res.1, f32[16,16,128]{2,1,0:T(8,128)} %stiff.1, f32[3,3]{1,0:T(4,128)S(1)} %copy-done), custom_call_target="tpu_custom_call" | custom-call | tf_op jit(solution)/shard_map/pallas_call | solution.py:673
  40.4 0.8 %maximum_add_fusion = f32[3,16,16,128]{3,2,1,0:T(8,128)} fusion(f32[3,16,16,128]{3,2,1,0:T(8,128)S(1)} %bitcast.9, f32[1,16,16,128]{3,2,1,0:T(8,128)S(1)} %bitcast.7, f32[1,16,16,128]{3,2,1,0:T(8,128)S(1)} %bitcast.6, f32[1,16,16,128]{3,2,1,0:T(8,128)S(1)} %bitcast.5), kind=kLoop, calls=%fused_computation | loop fusion | flops 294912 | bytes 1179648 | tf_op jit(solution)/shard_map/add | solution.py:689
  (2 shorter events, 0.0 us)
Async XLA Ops:
  0.0 0.7 %copy-start = (f32[3,3]{1,0:T(4,128)S(1)}, f32[3,3]{1,0:T(4,128)}, u32[]{:S(2)}) copy-start(f32[3,3]{1,0:T(4,128)} %coup_hbm.1) | copy-start | bytes 112
